TPU v7x, 32 devices: a whole 2x2x4 slice. The times are simulated.
32 devices in a mesh: parts: 1, dev: 32 (over z, y, x, core).
Axes of the slice: x: 2, y: 2, z: 4, core: 2. Of those that a mesh axis runs over, the one named last changes fastest.
Arguments:
- prompt_state: bfloat16 [32, 16, 128, 128], P(('parts', 'dev')), may hold values from -4 to 4
- conv_state: bfloat16 [32, 3, 4096], P(('parts', 'dev')), may hold values from -6 to 6
- slot_prompt: int32 [512], P(('parts', 'dev')), may hold values from 0 to 31, as said below
- mixed_input: bfloat16 [3, 512, 4096], P(None, ('parts', 'dev')), may hold values from -6 to 6
- output_gate: bfloat16 [3, 512, 2048], P(None, ('parts', 'dev')), may hold values from -6 to 6
- residual: bfloat16 [3, 512, 2048], P(None, ('parts', 'dev')), may hold values from -6 to 6
- beta_logit: float32 [3, 512, 16], P(None, ('parts', 'dev')), may hold values from -6 to 6
- decay_logit: float32 [3, 512, 16], P(None, ('parts', 'dev')), may hold values from -6 to 6
- decay_base: float32 [16], replicated, may hold values from -3 to 0.5
- decay_bias: float32 [16], replicated, may hold values from -2 to 0
- head_gain: float32 [128], replicated, may hold values from 0.1 to 1.9
- conv_weight: float32 [4, 4096], replicated, may hold values from -3 to 3
- out_weight: bfloat16 [2048, 2048], replicated, may hold values from -0.125 to 0.125
- post_gain: float32 [2048], replicated, may hold values from 0.1 to 1.9
- router: bfloat16 [2048, 32], replicated, may hold values from -0.375 to 0.375
- expert_gate: bfloat16 [32, 2048, 256], P('dev'), may hold values from -0.125 to 0.125
- expert_up: bfloat16 [32, 2048, 256], P('dev'), may hold values from -0.125 to 0.125
- expert_down: bfloat16 [32, 256, 2048], P('dev'), may hold values from -0.75 to 0.75
- route_ids: int32 [3, 512, 10], P(None, ('parts', 'dev')), may hold values from 0 to 31, all different within a row; in each aligned block of 16 rows (0 to 15, 16 to 31, ..., all dimensions but the last counted through in order) at most 10 rows name the same one
Outputs:
- layer_out: bfloat16 [3, 512, 2048], P(None, ('parts', 'dev'))
Inputs may be any that keep to these rules, and one draw needn't show every extreme that they name: `slot_prompt`: prompt p is held by device p. The 16 slots of device d hold samples of prompts d - 1, d and d + 1 only; every device with both neighbours holds 1 to 9 samples of each neighbour's prompt; every prompt has 8 to 32 samples, some prompt exactly 8 and some exactly 32. `route_ids`: each row names 10 different experts. At one step the rows of one device name one expert at most 10 times, a bound that some block reaches at some step and device.
All inputs are finite; a program needn't handle non-finite values.
Results may differ from a plain program's by a relative error of at most 0.0052.
Values may be sent and summed in bfloat16 or wider, within the bound.
A program may use at most 128 MiB of HBM per device.

v0:
```python
import math

import jax
import jax.numpy as jnp
from jax import lax
from jax.sharding import PartitionSpec as P

VH = 16
KH = 8
DK = 128
DV = 128


epsilon = 1e-06


def extended(block, sides, width):
    for axis, dim in sides:
        count = lax.axis_size(axis)
        forward = [(i, i + 1) for i in range(count - 1)]
        backward = [(target, source) for source, target in forward]
        low = lax.ppermute(
            lax.slice_in_dim(block, block.shape[dim] - width, None, axis=dim), axis, forward
        )
        high = lax.ppermute(lax.slice_in_dim(block, 0, width, axis=dim), axis, backward)
        block = jnp.concatenate([low, block, high], axis=dim)
    return block


def conv_advance(conv_rows, incoming, conv_weight):
    window = jnp.concatenate([conv_rows, incoming[:, None, :]], axis=1)
    activated = jax.nn.silu(jnp.sum(window * conv_weight[None], axis=1))
    return (window[:, 1:], activated)


def delta_advance(
    memory, activated, output_gate, beta_logit, decay_logit, decay_base, decay_bias, head_gain
):
    batch_size = activated.shape[0]
    key_width = KH * DK
    query_vec = activated[:, :key_width].reshape(batch_size, KH, DK)
    key_vec = activated[:, key_width : 2 * key_width].reshape(batch_size, KH, DK)
    value_vec = activated[:, 2 * key_width :].reshape(batch_size, VH, DV)
    query_vec = (
        query_vec
        * lax.rsqrt(jnp.sum(query_vec * query_vec, axis=-1, keepdims=True) + epsilon)
        * (1.0 / math.sqrt(DK))
    )
    key_vec = key_vec * lax.rsqrt(jnp.sum(key_vec * key_vec, axis=-1, keepdims=True) + epsilon)
    query_vec = jnp.repeat(query_vec, VH // KH, axis=1)
    key_vec = jnp.repeat(key_vec, VH // KH, axis=1)
    strength = jax.nn.sigmoid(beta_logit)
    retain = jnp.exp(-jnp.exp(decay_base) * jax.nn.softplus(decay_logit + decay_bias))
    memory = memory * retain[:, :, None, None]
    recalled = jnp.sum(memory * key_vec[..., None], axis=2)
    update = strength[..., None] * (value_vec - recalled)
    memory = memory + key_vec[..., None] * update[:, :, None, :]
    readout = jnp.sum(memory * query_vec[..., None], axis=2)
    readout = (
        readout
        * lax.rsqrt(jnp.mean(readout * readout, axis=-1, keepdims=True) + epsilon)
        * head_gain
    )
    readout = readout * jax.nn.silu(output_gate.astype(jnp.float32).reshape(batch_size, VH, DV))
    return (memory, readout.reshape(batch_size, VH * DV).astype(jnp.bfloat16))


def residual_norm(carried, post_gain):
    scaled = (
        carried
        * lax.rsqrt(jnp.mean(carried * carried, axis=-1, keepdims=True) + epsilon)
        * post_gain
    )
    return scaled.astype(jnp.bfloat16)


def expert_return(arrived, expert_gate, expert_up, expert_down):
    sources, item_count, model_width = arrived.shape
    flat_rows = arrived.reshape(sources * item_count, model_width)
    hidden = jax.nn.silu(jnp.dot(flat_rows, expert_gate[0], preferred_element_type=jnp.float32))
    hidden = (hidden * jnp.dot(flat_rows, expert_up[0], preferred_element_type=jnp.float32)).astype(
        jnp.bfloat16
    )
    result = jnp.dot(hidden, expert_down[0], preferred_element_type=jnp.float32).astype(
        jnp.bfloat16
    )
    result = result.reshape(sources, item_count, model_width)
    return lax.all_to_all(result, "dev", split_axis=0, concat_axis=0, tiled=True)


def expert_mixture(normed, chosen_ids, router, expert_gate, expert_up, expert_down):
    groups, slot_count, model_width = normed.shape
    top_count = chosen_ids.shape[2]
    experts = router.shape[1]
    capacity = min(slot_count, max(4, 2 * ((slot_count * top_count + experts - 1) // experts)))
    logits = jnp.dot(
        normed.reshape(groups * slot_count, model_width), router, preferred_element_type=jnp.float32
    )
    logits = logits.reshape(groups, slot_count, experts)
    chosen_hot = (chosen_ids[..., None] == jnp.arange(experts, dtype=jnp.int32)).astype(jnp.float32)
    chosen_logit = jnp.sum(chosen_hot * logits[:, :, None, :], axis=3)
    gate_value = jax.nn.sigmoid(chosen_logit)
    weights = gate_value / jnp.sum(gate_value, axis=2, keepdims=True)
    routed = jnp.sum(chosen_hot, axis=2)
    position = jnp.cumsum(routed, axis=1) - 1.0
    slot_range = jnp.arange(capacity, dtype=jnp.float32)
    every_token, every_mask = (
        lax.all_gather(normed, "dev", axis=1, tiled=True),
        lax.all_gather(routed.astype(jnp.bfloat16), "dev", axis=1, tiled=True),
    )
    devices = every_token.shape[1] // slot_count
    own_mask = lax.dynamic_slice_in_dim(every_mask, lax.axis_index("dev"), 1, 2)[..., 0].astype(
        jnp.float32
    )
    own_mask = own_mask.reshape(groups, devices, slot_count)
    own_position = jnp.cumsum(own_mask, axis=2) - 1.0
    taker_hot = (
        own_mask[..., None] * (own_position[..., None] == slot_range).astype(jnp.float32)
    ).astype(jnp.bfloat16)
    arrived = jnp.einsum(
        "gnsc,gnsd->ngcd",
        taker_hot,
        every_token.reshape(groups, devices, slot_count, model_width),
        preferred_element_type=jnp.float32,
    )
    arrived = arrived.astype(jnp.bfloat16).reshape(devices, groups * capacity, model_width)
    returned = expert_return(arrived, expert_gate, expert_up, expert_down)
    returned = returned.reshape(experts, groups, capacity, model_width)
    route_hot = chosen_hot[..., None] * (position[:, :, None, :, None] == slot_range).astype(
        jnp.float32
    )
    picked = jnp.einsum(
        "gskec,egcd->gskd",
        route_hot.astype(jnp.bfloat16),
        returned,
        preferred_element_type=jnp.float32,
    )
    return jnp.sum(weights[..., None] * picked, axis=2)


def body(
    prompt_state,
    conv_state,
    slot_prompt,
    mixed_input,
    output_gate,
    residual,
    beta_logit,
    decay_logit,
    decay_base,
    decay_bias,
    head_gain,
    conv_weight,
    out_weight,
    post_gain,
    router,
    expert_gate,
    expert_up,
    expert_down,
    route_ids,
):
    slot_count = slot_prompt.shape[0]
    step_count = mixed_input.shape[0]
    column = prompt_state.shape[3]
    state_rows = prompt_state.shape[1] * prompt_state.shape[2]
    packed = jnp.concatenate(
        [prompt_state.reshape(1, state_rows, column), conv_state.reshape(1, -1, column)], axis=1
    )
    nearby = extended(packed, (("dev", 0),), 1)
    offset = slot_prompt - (lax.axis_index("dev") - 1)
    chooser = (offset[:, None] == jnp.arange(3, dtype=jnp.int32)[None, :]).astype(jnp.bfloat16)
    opened = jnp.einsum("sp,prc->src", chooser, nearby, preferred_element_type=jnp.float32)
    memory = opened[:, :state_rows].reshape((slot_count,) + prompt_state.shape[1:])
    conv_rows = opened[:, state_rows:].reshape((slot_count,) + conv_state.shape[1:])
    carried_list = []
    normed_list = []
    for step_index in range(step_count):
        conv_rows, activated = conv_advance(
            conv_rows, mixed_input[step_index].astype(jnp.float32), conv_weight
        )
        memory, gated_out = delta_advance(
            memory,
            activated,
            output_gate[step_index],
            beta_logit[step_index],
            decay_logit[step_index],
            decay_base,
            decay_bias,
            head_gain,
        )
        carried = residual[step_index].astype(jnp.float32) + jnp.dot(
            gated_out, out_weight, preferred_element_type=jnp.float32
        )
        normed = residual_norm(carried, post_gain)
        carried_list.append(carried)
        normed_list.append(normed)
    mixture = expert_mixture(
        jnp.stack(normed_list), route_ids, router, expert_gate, expert_up, expert_down
    )
    layer_out = (jnp.stack(carried_list) + mixture).astype(jnp.bfloat16)
    return layer_out


def solution(mesh):
    in_specs = (
        P(("parts", "dev"), None, None, None),
        P(("parts", "dev"), None, None),
        P(("parts", "dev")),
        P(None, ("parts", "dev"), None),
        P(None, ("parts", "dev"), None),
        P(None, ("parts", "dev"), None),
        P(None, ("parts", "dev"), None),
        P(None, ("parts", "dev"), None),
        P(),
        P(),
        P(),
        P(),
        P(),
        P(),
        P(),
        P("dev", None, None),
        P("dev", None, None),
        P("dev", None, None),
        P(None, ("parts", "dev"), None),
    )
    out_specs = P(None, ("parts", "dev"), None)
    return jax.shard_map(body, mesh=mesh, in_specs=in_specs, out_specs=out_specs, check_vma=False)
```

profile of v0, /device:TPU:0, one launch (start us, length us, event | category | flops | bytes accessed | tf_op | source)
XLA Modules:
  0.0 349.8 jit_solution(15524594519907571239)
XLA Ops:
  6.5 1.9 copy_dynamic-update-slice_fusion
  8.4 0.8 reshape.470
  9.4 3.2 collective-permute-start
  12.5 1.3 collective-permute-start.1
  13.8 1.1 fusion.96
  15.2 0.7 exponential_negate_fusion
  15.8 1.2 fusion.37
  17.1 0.8 fusion.86
  17.8 0.7 divide_bitcast_fusion
  18.7 0.7 copy.98
  19.4 0.7 copy.105
  20.1 0.6 copy.109
  20.7 0.7 copy.112
  21.4 0.7 broadcast_subtract_fusion
  22.0 1.2 broadcast_bitcast_fusion
  23.3 5.5 %copy.92 = bf16[1,2144,128]{2,0,1:T(2,128)(2,1)S(1)} copy(bf16[1,2144,128]{2,1,0:T(8,128)(2,1)} %collective-permute-done) | data formatting | bytes 1097728 | tf_op jit(solution)/shard_map/ppermute | solution.py:22
  28.8 5.7 %copy.93 = bf16[1,2144,128]{2,0,1:T(2,128)(2,1)S(1)} copy(bf16[1,2144,128]{2,1,0:T(8,128)(2,1)} %collective-permute-done.1) | data formatting | bytes 1097728 | tf_op jit(solution)/shard_map/ppermute | solution.py:25
  34.5 4.5 %fusion.6 = f32[16,2144,128]{2,0,1:T(8,128)S(1)} fusion(bf16[1,2144,128]{2,0,1:T(2,128)(2,1)S(1)} %copy.93, bf16[1,2144,128]{2,0,1:T(2,128)(2,1)S(1)} %constant_dynamic-update-slice_fusion, bf16[1,2144,128]{2,0,1:T(2,128)(2,1)S(1)} %copy.92, s32[16]{0:T(128)S(1)} %broadcast_subtract_fusion), kind=kOutput, calls=%fused_computation.18 | convolution fusion | flops 31285296 | bytes 19210304 | tf_op jit(solution)/shard_map/sp,prc->src/dot_general | solution.py:172
  39.1 6.0 %copy-done.1 = f32[16,2144,128]{2,0,1:T(8,128)} copy-done((f32[16,2144,128]{2,0,1:T(8,128)}, f32[16,2144,128]{2,0,1:T(8,128)S(1)}, u32[]{:S(2)}) %copy-start.1) | copy-done | bytes 17563672
  45.7 0.6 fusion.20
  46.3 0.6 fusion.17
  46.9 3.9 %fusion.19 = (f32[16,4096]{1,0:T(8,128)S(1)}, f32[16,4096]{1,0:T(8,128)S(1)}, f32[16,4096]{1,0:T(8,128)S(1)}) fusion(f32[16,1,4096]{2,1,0:T(1,128)S(1)} %fusion.39, f32[16,3,4096]{2,1,0:T(4,128)S(1)} %reshape.443, f32[4,4096]{1,0:T(4,128)S(1)} %copy-done.12, f32[16,1,4096]{2,1,0:T(1,128)S(1)} %get-tuple-element.39, f32[16,3,4096]{2,1,0:T(4,128)S(1)} %fusion.20, ...), kind=kLoop, calls=%fused_computation.36 | loop fusion | flops 2162688 | bytes 3997696 | tf_op jit(solution)/shard_map/reduce_sum | solution.py:32
  52.5 0.7 slice_bitcast_fusion.4
  53.6 0.9 copy.137
  54.7 1.0 copy.114
  55.9 1.0 copy.107
  57.1 10.4 %multiply_reduce_fusion.5 = f32[16,16,128]{2,0,1:T(8,128)S(1)} fusion(f32[16,2144,128]{2,0,1:T(8,128)} %copy-done.1, f32[16,16,128]{0,2,1:T(8,128)S(1)} %bitcast.218, f32[16,16]{0,1:T(8,128)S(1)} %copy.94), kind=kLoop, calls=%fused_computation.7 | loop fusion | flops 12550144 | bytes 17040384 | tf_op jit(solution)/shard_map/reduce_sum | solution.py:55
  67.9 17.3 %multiply_reduce_fusion.4 = (f32[16,16,128]{2,0,1:T(8,128)S(1)}, f32[16,16,128]{2,0,1:T(8,128)S(1)}) fusion(f32[16,16,128]{0,2,1:T(8,128)S(1)} %bitcast.230, f32[16,16,128]{2,0,1:T(8,128)S(1)} %fusion.56, f32[16,16,128]{0,2,1:T(8,128)S(1)} %bitcast.219, f32[16,16]{0,1:T(8,128)S(1)} %copy.94, f32[16,2144,128]{2,0,1:T(8,128)} %copy-done.1, ...), kind=kLoop, calls=%fused_computation.5 | loop fusion | flops 33488896 | bytes 17565696 | tf_op jit(solution)/shard_map/reduce_sum | solution.py:58
  85.6 16.0 %multiply_reduce_fusion.1 = f32[16,16,128]{2,0,1:T(8,128)S(1)} fusion(f32[16,16,128]{0,2,1:T(8,128)S(1)} %bitcast.225, f32[16,16]{0,1:T(8,128)S(1)} %copy-done.11, f32[16,16,128]{2,0,1:T(8,128)S(1)} %fusion.55, f32[16,16,128]{0,2,1:T(8,128)S(1)} %bitcast.223, f32[16,16]{0,1:T(8,128)S(1)} %copy.102, f32[16,16,128]{2,0,1:T(8,128)S(1)} %fusion.56, ...), kind=kLoop, calls=%fused_computation.1 | loop fusion | flops 37715968 | bytes 17566720 | tf_op jit(solution)/shard_map/reduce_sum | solution.py:55
  102.0 24.8 %multiply_reduce_fusion.2 = (f32[16,16,128]{2,0,1:T(8,128)S(1)}, f32[16,16,128]{2,0,1:T(8,128)S(1)}) fusion(f32[16,16,128]{0,2,1:T(8,128)S(1)} %bitcast.229, f32[16,16,128]{2,0,1:T(8,128)S(1)} %fusion.55, f32[16,16,128]{0,2,1:T(8,128)S(1)} %bitcast.224, f32[16,16]{0,1:T(8,128)S(1)} %copy.102, f32[16,16,128]{2,0,1:T(8,128)S(1)} %fusion.56, ...), kind=kLoop, calls=%fused_computation.2 | loop fusion | flops 54460416 | bytes 18091008 | tf_op jit(solution)/shard_map/reduce_sum | solution.py:58
  127.0 1.3 multiply_reduce_fusion.6
  128.5 1.3 multiply_reduce_fusion.7
  130.0 1.3 multiply_reduce_fusion.8
  131.5 0.7 pad_maximum_fusion.2
  132.7 45.8 %all_gather.6 = bf16[3,512,32]{2,1,0:T(8,128)(2,1)S(1)} all-gather(bf16[3,16,32]{2,1,0:T(8,128)(2,1)S(1)} %convert_element_type.179), channel_id=1, replica_groups=mesh['parts'=1,'dev'=32] {'dev'}, dimensions={1}, use_global_device_ids=true | all-gather | bytes 101376 | tf_op jit(solution)/shard_map/all_gather | solution.py:109
  178.5 0.3 convert_reduce_fusion
  179.0 0.8 reduce_window_sum.23
  179.8 26.3 %all-gather.2.cloned.1.call-done = bf16[3,512,2048]{2,1,0:T(8,128)(2,1)} async-done(((bf16[3,16,2048]{2,1,0:T(8,128)(2,1)}), bf16[3,512,2048]{2,1,0:T(8,128)(2,1)}) %all-gather.2.cloned.1.call-update) | async-done | bytes 6291472 | tf_op jit(solution)/shard_map/all_gather | solution.py:108
  206.1 7.3 %fusion.2 = bf16[32,3,10,2048]{3,2,1,0:T(8,128)(2,1)} fusion(bf16[3,32,16,2048]{3,2,1,0:T(8,128)(2,1)} %bitcast.227, bf16[3,32,16]{2,0,1:T(4,128)(2,1)S(1)} %copy.118, f32[3,32,16]{2,0,1:T(4,128)S(1)} %copy.117), kind=kOutput, calls=%fused_computation.10 | convolution fusion | flops 64911360 | bytes 10232832 | tf_op jit(solution)/shard_map/gnsc,gnsd->ngcd/dot_general | solution.py:120
  213.4 7.5 %reshape_reshape.3 = bf16[960,2048]{1,0:T(8,128)(2,1)} reshape(bf16[32,3,10,2048]{3,2,1,0:T(8,128)(2,1)} %fusion.2) | data formatting | bytes 7864320 | tf_op jit(solution)/shard_map/reshape;reshape | solution.py:79
  220.9 4.3 %fusion.25 = f32[960,256]{1,0:T(8,128)} fusion(bf16[960,2048]{1,0:T(8,128)(2,1)} %reshape_reshape.3, bf16[1,2048,256]{2,1,0:T(8,128)(2,1)S(1)} %copy-done.18), kind=kOutput, calls=%fused_computation.42 | convolution fusion | flops 1006632960 | bytes 5963776 | tf_op jit(solution)/shard_map/dot_general | solution.py:80
  225.2 8.8 %convolution_convert_fusion = bf16[960,2048]{1,0:T(8,128)(2,1)} fusion(bf16[960,2048]{1,0:T(8,128)(2,1)} %reshape_reshape.3, bf16[1,256,2048]{2,1,0:T(8,128)(2,1)S(1)} %copy-done, bf16[1,2048,256]{2,1,0:T(8,128)(2,1)} %param.35, f32[960,256]{1,0:T(8,128)} %fusion.25), kind=kOutput, calls=%fused_computation.13 | convolution fusion | flops 2016706560 | bytes 10944512 | tf_op jit(solution)/shard_map/dot_general | solution.py:84
  234.0 5.0 %reshape.454 = bf16[32,30,2048]{2,1,0:T(8,128)(2,1)} reshape(bf16[960,2048]{1,0:T(8,128)(2,1)} %convolution_convert_fusion) | data formatting | bytes 7864320 | tf_op jit(solution)/shard_map/reshape | solution.py:87
  239.0 3.6 %all-to-all-start = ((bf16[32,30,2048]{2,1,0:T(8,128)(2,1)}), bf16[32,30,2048]{2,1,0:T(8,128)(2,1)}, u32[]{:S(2)}, u32[]{:S(2)}) async-start(bf16[32,30,2048]{2,1,0:T(8,128)(2,1)} %reshape.454), calls=%async_computation | async-start | bytes 8388608 | tf_op jit(solution)/shard_map/all_to_all | solution.py:88
  242.9 93.6 %all-to-all-done = bf16[32,30,2048]{2,1,0:T(8,128)(2,1)} async-done(((bf16[32,30,2048]{2,1,0:T(8,128)(2,1)}), bf16[32,30,2048]{2,1,0:T(8,128)(2,1)}, u32[]{:S(2)}, u32[]{:S(2)}) %all-to-all-start) | async-done | bytes 3932192 | tf_op jit(solution)/shard_map/all_to_all | solution.py:88
  336.5 4.3 %copy.120 = bf16[32,30,2048]{2,0,1:T(8,128)(2,1)S(1)} copy(bf16[32,30,2048]{2,1,0:T(8,128)(2,1)} %all-to-all-done) | data formatting | bytes 7864320 | tf_op jit(solution)/shard_map/all_to_all | solution.py:88
  340.9 1.3 fusion.5
  342.2 0.7 fusion.33
  (132 shorter events, 5.9 us)
Async XLA Ops:
  6.5 218.7 %copy-start = (bf16[1,256,2048]{2,1,0:T(8,128)(2,1)S(1)}, bf16[1,256,2048]{2,1,0:T(8,128)(2,1)}, u32[]{:S(2)}) copy-start(bf16[1,256,2048]{2,1,0:T(8,128)(2,1)} %param.36) | copy-start | bytes 3145732
  6.5 199.6 %all-gather.2.cloned.1.call-start = ((), (), s32[]{:S(2)}) async-start(), calls=%async_computation.1 | async-start | bytes 6488064 | tf_op jit(solution)/shard_map/all_gather | solution.py:108
  9.4 13.9 %collective-permute-start = (bf16[1,2144,128]{2,1,0:T(8,128)(2,1)S(1)}, bf16[1,2144,128]{2,1,0:T(8,128)(2,1)}, u32[]{:S(2)}, u32[]{:S(2)}) collective-permute-start(bf16[1,2144,128]{2,1,0:T(8,128)(2,1)S(1)} %copy.90), channel_id=1, source_target_pairs={{0,1},{1,2},{2,3},{3,4},{4,5},{5,6},{6,7},{7,8},{8,9},{9,10},{10,1... | collective-permute-start | bytes 1646600 | tf_op jit(solution)/shard_map/ppermute | solution.py:22
  12.5 16.3 %collective-permute-start.1 = (bf16[1,2144,128]{2,1,0:T(8,128)(2,1)S(1)}, bf16[1,2144,128]{2,1,0:T(8,128)(2,1)}, u32[]{:S(2)}, u32[]{:S(2)}) collective-permute-start(bf16[1,2144,128]{2,1,0:T(8,128)(2,1)S(1)} %copy.90), channel_id=1, source_target_pairs={{1,0},{2,1},{3,2},{4,3},{5,4},{6,5},{7,6},{8,7},{9,8},{10,9},{11,1... | collective-permute-start | bytes 1646600 | tf_op jit(solution)/shard_map/ppermute | solution.py:25
  39.1 6.0 %copy-start.1 = (f32[16,2144,128]{2,0,1:T(8,128)}, f32[16,2144,128]{2,0,1:T(8,128)S(1)}, u32[]{:S(2)}) copy-start(f32[16,2144,128]{2,0,1:T(8,128)S(1)} %fusion.6) | copy-start | bytes 52690948
  45.1 1.8 copy-start.12
  51.4 0.7 copy-start.4
  52.5 0.8 copy-start.6
  57.1 10.5 %copy-start.15 = (f32[16,16]{0,1:T(8,128)S(1)}, f32[16,16]{0,1:T(8,128)}, u32[]{:S(2)}) copy-start(f32[16,16]{0,1:T(8,128)} %copy.98) | copy-start | bytes 3076
  57.1 28.4 %slice-start = ((s8[17563648]{0:T(1024)(128)(4,1)}), s8[4194304]{0:T(1024)(128)(4,1)S(1)}, s32[]{:S(2)}) async-start(s8[17563648]{0:T(1024)(128)(4,1)} %bitcast.214), calls=%async_computation.2 | async-start | bytes 8388608
  57.1 28.4 %slice-start.1 = ((s8[17563648]{0:T(1024)(128)(4,1)}), s8[4194304]{0:T(1024)(128)(4,1)S(1)}, s32[]{:S(2)}) async-start(s8[17563648]{0:T(1024)(128)(4,1)} %bitcast.214), calls=%async_computation.3 | async-start | bytes 8388608
  57.1 28.4 %slice-start.2 = ((s8[17563648]{0:T(1024)(128)(4,1)}), s8[4194304]{0:T(1024)(128)(4,1)S(1)}, s32[]{:S(2)}) async-start(s8[17563648]{0:T(1024)(128)(4,1)} %bitcast.214), calls=%async_computation.4 | async-start | bytes 8388608
  67.9 17.4 %copy-start.5 = (f32[16,4096]{1,0:T(8,128)S(1)}, f32[16,4096]{1,0:T(8,128)}, u32[]{:S(2)}) copy-start(f32[16,4096]{1,0:T(8,128)} %copy-done.4) | copy-start | bytes 786436
  67.9 17.4 %copy-start.14 = (f32[16,16]{0,1:T(8,128)S(1)}, f32[16,16]{0,1:T(8,128)}, u32[]{:S(2)}) copy-start(f32[16,16]{0,1:T(8,128)} %copy.105) | copy-start | bytes 3076
  67.9 17.6 %slice-start.3 = ((s8[17563648]{0:T(1024)(128)(4,1)}), s8[4194304]{0:T(1024)(128)(4,1)S(1)}, s32[]{:S(2)}) async-start(s8[17563648]{0:T(1024)(128)(4,1)} %bitcast.214), calls=%async_computation.5 | async-start | bytes 8388608
  67.9 17.6 %slice-start.4 = ((s8[17563648]{0:T(1024)(128)(4,1)}), s8[786432]{0:T(1024)(128)(4,1)S(1)}, s32[]{:S(2)}) async-start(s8[17563648]{0:T(1024)(128)(4,1)} %bitcast.214), calls=%async_computation.6 | async-start | bytes 1572864
  67.9 17.6 %copy-start.11 = (f32[16,16]{0,1:T(8,128)S(1)}, f32[16,16]{0,1:T(8,128)}, u32[]{:S(2)}) copy-start(f32[16,16]{0,1:T(8,128)} %copy.109) | copy-start | bytes 3076
  85.6 16.0 %copy-start.7 = (f32[16,4096]{1,0:T(8,128)S(1)}, f32[16,4096]{1,0:T(8,128)}, u32[]{:S(2)}) copy-start(f32[16,4096]{1,0:T(8,128)} %copy-done.6) | copy-start | bytes 786436
  85.6 16.0 %copy-start.13 = (f32[16,16]{0,1:T(8,128)S(1)}, f32[16,16]{0,1:T(8,128)}, u32[]{:S(2)}) copy-start(f32[16,16]{0,1:T(8,128)} %copy.112) | copy-start | bytes 3076
  85.6 16.1 %copy-start.2 = (f32[16,8,128]{0,2,1:T(8,128)S(1)}, f32[16,8,128]{0,2,1:T(8,128)}, u32[]{:S(2)}) copy-start(f32[16,8,128]{0,2,1:T(8,128)} %copy.114) | copy-start | bytes 196612
  85.6 16.2 %copy-start.3 = (f32[16,8,128]{0,2,1:T(8,128)S(1)}, f32[16,8,128]{0,2,1:T(8,128)}, u32[]{:S(2)}) copy-start(f32[16,8,128]{0,2,1:T(8,128)} %copy.107) | copy-start | bytes 196612
  101.9 25.1 %slice-start.5 = ((s8[8388608]{0:T(1024)(128)(4,1)}), s8[4194304]{0:T(1024)(128)(4,1)S(1)}, s32[]{:S(2)}) async-start(s8[8388608]{0:T(1024)(128)(4,1)} %bitcast.216), calls=%async_computation.7 | async-start | bytes 8388608
  102.0 25.0 %slice-start.6 = ((s8[8388608]{0:T(1024)(128)(4,1)}), s8[4194304]{0:T(1024)(128)(4,1)S(1)}, s32[]{:S(2)}) async-start(s8[8388608]{0:T(1024)(128)(4,1)} %bitcast.216), calls=%async_computation.8 | async-start | bytes 8388608
  102.0 25.0 %copy-start.8 = (bf16[3,16,2048]{2,1,0:T(8,128)(2,1)S(1)}, bf16[3,16,2048]{2,1,0:T(8,128)(2,1)}, u32[]{:S(2)}) copy-start(bf16[3,16,2048]{2,1,0:T(8,128)(2,1)} %param.23) | copy-start | bytes 589828
  102.0 25.0 %copy-start.9 = (bf16[3,16,2048]{2,1,0:T(8,128)(2,1)S(1)}, bf16[3,16,2048]{2,1,0:T(8,128)(2,1)}, u32[]{:S(2)}) copy-start(bf16[3,16,2048]{2,1,0:T(8,128)(2,1)} %param.24) | copy-start | bytes 589828
  102.0 25.0 %copy-start.10 = (f32[2048]{0:T(1024)S(1)}, f32[2048]{0:T(1024)}, u32[]{:S(2)}) copy-start(f32[2048]{0:T(1024)} %broadcast_bitcast_fusion) | copy-start | bytes 24580
  128.5 2.9 copy-start.17
  128.5 3.7 %copy-start.16 = (s32[3,16,10]{1,0,2:T(4,128)S(1)}, s32[3,16,10]{1,0,2:T(4,128)}, u32[]{:S(2)}) copy-start(s32[3,16,10]{1,0,2:T(4,128)} %param.37) | copy-start | bytes 5764
  128.5 3.7 %copy-start.19 = (bf16[2048,32]{0,1:T(8,128)(2,1)S(1)}, bf16[2048,32]{0,1:T(8,128)(2,1)}, u32[]{:S(2)}) copy-start(bf16[2048,32]{0,1:T(8,128)(2,1)} %param.33) | copy-start | bytes 393220
  206.1 14.8 %copy-start.18 = (bf16[1,2048,256]{2,1,0:T(8,128)(2,1)S(1)}, bf16[1,2048,256]{2,1,0:T(8,128)(2,1)}, u32[]{:S(2)}) copy-start(bf16[1,2048,256]{2,1,0:T(8,128)(2,1)} %param.34) | copy-start | bytes 3145732
  239.0 97.5 %all-to-all-start = ((bf16[32,30,2048]{2,1,0:T(8,128)(2,1)}), bf16[32,30,2048]{2,1,0:T(8,128)(2,1)}, u32[]{:S(2)}, u32[]{:S(2)}) async-start(bf16[32,30,2048]{2,1,0:T(8,128)(2,1)} %reshape.454), calls=%async_computation | async-start | bytes 8388608 | tf_op jit(solution)/shard_map/all_to_all | solution.py:88
Sparse Core Ops, SparseCore 0:
  132.4 73.6 all-gather.1
where the time goes:
time: 351 us; the launch traced here: 350 us
  waiting for transfers between devices  120 us (34%)
  other arithmetic  83 us (24%)
  local copies, waits for them, and re-layouts  48.2 us (14%)
  blocking collectives  45.8 us (13%)
  matrix products  30.5 us (9%)
  between operations  14.4 us (4%)
  starting transfers between devices  8.09 us (2%)
    all_to_all x1, waiting for transfers between devices, expert_return(): lax.all_to_all(result, 'dev', split_axis=0, concat_axis=0, tiled=True)  93.6 us
    all_gather x1, blocking collectives, expert_mixture(): lax.all_gather(routed.astype(jnp.bfloat16), 'dev', axis=1, tiled=True)  45.8 us
    reduce_sum x2, other arithmetic, delta_advance(): readout = jnp.sum(memory * query_vec[..., None], axis=2)  42.1 us
    reduce_sum x2, other arithmetic, delta_advance(): recalled = jnp.sum(memory * key_vec[..., None], axis=2)  26.4 us
    all_gather x1, waiting for transfers between devices, expert_mixture(): lax.all_gather(normed, 'dev', axis=1, tiled=True)  26.3 us
    unnamed x65, local copies, waits for them, and re-layouts  9.78 us
    dot_general x1, matrix products, expert_return(): jnp.dot(hidden, expert_down[0], preferred_element_type=jnp.float32)  8.78 us
    another operation x1, local copies, waits for them, and re-layouts, expert_return(): flat_rows = arrived.reshape(sources * item_count, model_width)  7.51 us
  transfers between devices with their start and end apart: 4, of which 2 were waited for; matrix products, arithmetic and copies ran while one was open for 5% of the time, Pallas kernels for 0%

commit v1 on v0

v1 whole, which is shorter than its diff:
```python
import math

import jax
import jax.numpy as jnp
from jax import lax
from jax.experimental import pallas as pl
from jax.experimental.pallas import tpu as pltpu
from jax.sharding import PartitionSpec as P

epsilon = 1e-06


def halves(x):
    high = lax.reduce_precision(x, 8, 7)
    return high, x - high


def delta_kernel(
    offset_ref, low_state, own_state, high_state, low_conv, own_conv, high_conv,
    mixed_ref, gate_ref, strength_ref, retain_ref, gain_ref, weight_ref, out_ref,
):
    steps, slots, _ = mixed_ref.shape
    heads, key_size, value_size = own_state.shape[1:]
    taps, channels = weight_ref.shape
    key_heads = (channels - heads * value_size) // (2 * key_size)
    share = heads // key_heads
    key_width = key_heads * key_size
    offset = offset_ref[...]
    is_low, is_high = offset == 0, offset == 2
    all_low = jnp.concatenate([is_low] * (4 * steps), axis=0)
    all_high = jnp.concatenate([is_high] * (4 * steps), axis=0)
    gain = gain_ref[...]

    def convolved(start, width):
        columns = slice(start, start + width)
        rows = []
        for j in range(taps - 1):
            own, low, high = (
                r[0, j : j + 1, columns].astype(jnp.float32) for r in (own_conv, low_conv, high_conv)
            )
            rows.append(jnp.where(is_low, low, jnp.where(is_high, high, own)))
        for t in range(steps):
            rows.append(mixed_ref[t, :, columns].astype(jnp.float32))
        results = []
        for t in range(steps):
            total = rows[t] * weight_ref[0:1, columns]
            for j in range(1, taps):
                total = total + rows[t + j] * weight_ref[j : j + 1, columns]
            results.append(total * jax.nn.sigmoid(total))
        return results

    def summed(x):
        return jnp.sum(x, axis=-1, keepdims=True)

    for group in range(key_heads):
        query = [
            x * (lax.rsqrt(summed(x * x) + epsilon) * (1.0 / math.sqrt(key_size)))
            for x in convolved(group * key_size, key_size)
        ]
        key = [
            x * lax.rsqrt(summed(x * x) + epsilon)
            for x in convolved(key_width + group * key_size, key_size)
        ]
        parts = []
        for x in query + key:
            high = x.astype(jnp.bfloat16)
            parts += [high, (x - high.astype(jnp.float32)).astype(jnp.bfloat16)]
        stacked = jnp.concatenate(parts, axis=0)
        query_key = [[summed(query[t] * key[j]) for j in range(t + 1)] for t in range(steps)]
        key_key = [[summed(key[t] * key[j]) for j in range(t)] for t in range(steps)]
        for head in range(group * share, (group + 1) * share):
            low, own, high = (
                jnp.dot(stacked, r[0, head], preferred_element_type=jnp.float32)
                for r in (low_state, own_state, high_state)
            )
            product = jnp.where(all_low, low, jnp.where(all_high, high, own))
            read = [
                product[2 * i * slots : (2 * i + 1) * slots]
                + product[(2 * i + 1) * slots : (2 * i + 2) * slots]
                for i in range(2 * steps)
            ]
            value = convolved(2 * key_width + head * value_size, value_size)
            columns = slice(head * value_size, (head + 1) * value_size)
            updates = []
            for t in range(steps):
                recalled, readout = read[steps + t], read[t]
                for j in range(t + 1):
                    retain = retain_ref[j, :, head : head + 1]
                    recalled, readout = recalled * retain, readout * retain
                    if j < t:
                        recalled = recalled + key_key[t][j] * updates[j]
                        readout = readout + query_key[t][j] * updates[j]
                update = strength_ref[t, :, head : head + 1] * (value[t] - recalled)
                updates.append(update)
                readout = readout + query_key[t][t] * update
                readout = (
                    readout
                    * lax.rsqrt(summed(readout * readout) * (1.0 / value_size) + epsilon)
                    * gain
                )
                opened = gate_ref[t, :, columns].astype(jnp.float32)
                readout = readout * (opened * jax.nn.sigmoid(opened))
                out_ref[t * slots : (t + 1) * slots, columns] = readout.astype(out_ref.dtype)


def body(
    prompt_state, conv_state, slot_prompt, mixed_input, output_gate, residual, beta_logit,
    decay_logit, decay_base, decay_bias, head_gain, conv_weight, out_weight, post_gain, router,
    expert_gate, expert_up, expert_down, route_ids,
):
    steps, slots, width = residual.shape
    count = lax.axis_size("dev")
    me = lax.axis_index("dev")
    rows = steps * slots
    forward = [(i, i + 1) for i in range(count - 1)]
    backward = [(i + 1, i) for i in range(count - 1)]
    low_conv = lax.ppermute(conv_state, "dev", forward)
    high_conv = lax.ppermute(conv_state, "dev", backward)
    low_state = lax.ppermute(prompt_state, "dev", forward)
    high_state = lax.ppermute(prompt_state, "dev", backward)
    offset = (slot_prompt - (me - 1)).reshape(slots, 1)
    strength = jax.nn.sigmoid(beta_logit)
    retain = jnp.exp(-jnp.exp(decay_base) * jax.nn.softplus(decay_logit + decay_bias))
    heads, value_size = prompt_state.shape[1], prompt_state.shape[3]
    gated = pl.pallas_call(
        delta_kernel,
        out_shape=jax.ShapeDtypeStruct((rows, heads * value_size), jnp.bfloat16),
        in_specs=[pl.BlockSpec(memory_space=pltpu.VMEM)] * 13,
        out_specs=pl.BlockSpec(memory_space=pltpu.VMEM),
        compiler_params=pltpu.CompilerParams(vmem_limit_bytes=24 * 1024 * 1024),
    )(
        offset, low_state, prompt_state, high_state, low_conv, conv_state, high_conv,
        mixed_input, output_gate, strength, retain, head_gain.reshape(1, -1), conv_weight,
    )
    carried = residual.reshape(rows, width).astype(jnp.float32) + jnp.dot(
        gated, out_weight, preferred_element_type=jnp.float32
    )
    normed = (
        carried
        * lax.rsqrt(jnp.mean(carried * carried, axis=-1, keepdims=True) + epsilon)
        * post_gain
    ).astype(jnp.bfloat16)
    experts = router.shape[1]
    logits = jnp.dot(normed, router, preferred_element_type=jnp.float32)
    chosen = jnp.any(
        route_ids.reshape(rows, -1, 1) == jnp.arange(experts, dtype=jnp.int32), axis=1
    )
    weights = jnp.where(chosen, jax.nn.sigmoid(logits), 0.0)
    weights = weights / jnp.sum(weights, axis=1, keepdims=True)
    high, low = halves(weights)
    extra = -(-2 * experts // 128) * 128
    tail = jnp.concatenate(
        [high, low, jnp.zeros((rows, extra - 2 * experts), jnp.float32)], axis=1
    ).astype(jnp.bfloat16)
    gathered = lax.all_gather(jnp.concatenate([normed, tail], axis=1), "dev", axis=0, tiled=True)
    tokens = gathered[:, :width]
    column = jnp.arange(extra, dtype=jnp.int32)
    mine = (column == me) | (column == me + experts)
    weight = jnp.sum(
        jnp.where(mine, gathered[:, width:].astype(jnp.float32), 0.0), axis=1, keepdims=True
    )
    hidden = jax.nn.silu(jnp.dot(tokens, expert_gate[0], preferred_element_type=jnp.float32))
    hidden = hidden * jnp.dot(tokens, expert_up[0], preferred_element_type=jnp.float32)
    result = jnp.dot(
        hidden.astype(jnp.bfloat16), expert_down[0], preferred_element_type=jnp.float32
    )
    result = (result * weight).astype(jnp.bfloat16)
    mixture = lax.psum_scatter(result, "dev", scatter_dimension=0, tiled=True)
    layer_out = (carried + mixture.astype(jnp.float32)).astype(jnp.bfloat16)
    return layer_out.reshape(steps, slots, width)


def solution(mesh):
    split = P(None, ("parts", "dev"), None)
    in_specs = (
        P(("parts", "dev"), None, None, None),
        P(("parts", "dev"), None, None),
        P(("parts", "dev")),
        split, split, split, split, split,
        P(), P(), P(), P(), P(), P(), P(),
        P("dev", None, None),
        P("dev", None, None),
        P("dev", None, None),
        split,
    )
    return jax.shard_map(body, mesh=mesh, in_specs=in_specs, out_specs=split, check_vma=False)
```

time: 351 us -> 261 us (0.74)
  other arithmetic: 83 us -> 5.18 us
  waiting for transfers between devices: 120 us -> 197 us
  blocking collectives: 45.8 us -> 0 us
  local copies, waits for them, and re-layouts: 48.2 us -> 7.03 us
  matrix products: 30.5 us -> 21.7 us
  Pallas kernels: 0 us -> 5.63 us
    reduce_scatter x0 -> x1, waiting for transfers between devices: none -> 113 us  [body(): mixture = lax.psum_scatter(result, 'dev', scatter_dimension=0, tiled=True)]
    all_to_all x1 -> x0, waiting for transfers between devices: 93.6 us -> none  [expert_return(): lax.all_to_all(result, 'dev', split_axis=0, concat_axis=0, tiled=True)]
    reduce_sum x16 -> x1, other arithmetic: 73.6 us -> 1.18 us  [body(): jnp.sum(jnp.where(mine, gathered[:, width:].astype(jnp.float32), 0.0), ax...]
    all_gather x1, waiting for transfers between devices: 26.3 us -> 83 us  [body(): lax.all_gather(jnp.concatenate([normed, tail], axis=1), 'dev', axis=0, ti...]
    all_gather x1 -> x0, blocking collectives: 45.8 us -> none  [expert_mixture(): lax.all_gather(routed.astype(jnp.bfloat16), 'dev', axis=1, tiled=True)]
    ppermute x2 -> x0, local copies, waits for them, and re-layouts: 11.2 us -> none  [the longest x1 5.7 us: extended(): lax.ppermute(lax.slice_in_dim(block, 0, width, axis=dim), axis, backward)]
    dot_general x9 -> x4, matrix products: 30.5 us -> 21.7 us  [the longest x1 10.5 us: body(): jnp.dot(hidden.astype(jnp.bfloat16), expert_down[0], preferred_element_ty...]
    another operation x1 -> x0, local copies, waits for them, and re-layouts: 7.51 us -> none  [expert_return(): flat_rows = arrived.reshape(sources * item_count, model_width)]
  transfers between devices with their start and end apart: 4 -> 6, of which waited for: 2 -> 3; matrix products, arithmetic and copies ran while one was open for 5% -> 1% of each run, Pallas kernels for 0% -> 0%
where the time goes in v1:
time: 261 us; the launch traced here: 260 us
  waiting for transfers between devices  197 us (75%)
  matrix products  21.7 us (8%)
  between operations  13.6 us (5%)
  starting transfers between devices  10.3 us (4%)
  local copies, waits for them, and re-layouts  7.03 us (3%)
  Pallas kernels  5.63 us (2%)
  other arithmetic  5.18 us (2%)
    reduce_scatter x1, waiting for transfers between devices, body(): mixture = lax.psum_scatter(result, 'dev', scatter_dimension=0, tiled=True)  113 us
    all_gather x1, waiting for transfers between devices, body(): lax.all_gather(jnp.concatenate([normed, tail], axis=1), 'dev', axis=0, ti...  83 us
    dot_general x1, matrix products, body(): jnp.dot(hidden.astype(jnp.bfloat16), expert_down[0], preferred_element_ty...  10.5 us
    dot_general x1, matrix products, body(): jnp.dot(tokens, expert_gate[0], preferred_element_type=jnp.float32)  5.82 us
    pallas_call x1, Pallas kernels, body(): pl.pallas_call(delta_kernel, out_shape=jax.ShapeDtypeStruct((rows, heads...  5.63 us
    unnamed x22, local copies, waits for them, and re-layouts  5.24 us
  transfers between devices with their start and end apart: 6, of which 3 were waited for; matrix products, arithmetic and copies ran while one was open for 1% of the time, Pallas kernels for 0%

profile of v1, /device:TPU:0, one launch (start us, length us, event | category | flops | bytes accessed | tf_op | source)
XLA Modules:
  0.0 260.2 jit_solution(18096391492660519325)
XLA Ops:
  6.5 0.0 copy-start
  6.5 0.0 all-gather.2.cloned.1.call-start
  6.5 2.5 collective-permute-start.2
  9.0 1.3 collective-permute-start.3
  10.3 5.2 %collective-permute-start = (bf16[1,16,128,128]{3,2,1,0:T(8,128)(2,1)}, bf16[1,16,128,128]{3,2,1,0:T(8,128)(2,1)S(1)}, u32[]{:S(2)}, u32[]{:S(2)}) collective-permute-start(bf16[1,16,128,128]{3,2,1,0:T(8,128)(2,1)} %own_state.1), channel_id=1, source_target_pairs={{0,1},{1,2},{2,3},{3,4},{4,5},{5,6},{6,7},{7,8},{8,9},{9,10},{10,1... | collective-permute-start | bytes 1572872 | tf_op jit(solution)/shard_map/ppermute | solution.py:119
  15.5 1.3 collective-permute-start.1
  16.8 0.7 exponential_negate_fusion
  17.5 0.8 eq.27
  18.3 0.7 subtract_bitcast_fusion
  18.9 0.8 fusion.24
  19.8 0.1 copy.26.offset_ref
  19.9 0.1 copy.28
  20.0 0.0 collective-permute-done.2.low_conv
  20.0 0.0 collective-permute-done.3.high_conv
  20.0 0.0 collective-permute-done.low_state
  20.0 0.7 collective-permute-done.1.high_state
  20.7 0.0 copy-start.1
  20.7 1.0 copy-done.1
  21.8 0.0 copy-start.2
  21.8 1.0 copy-done.2
  22.8 0.9 copy-done.3
  23.7 0.8 copy-done.4
  24.5 0.8 copy-done.5
  25.3 0.7 copy-done.6
  26.0 5.6 %shard_map.181 = bf16[48,2048]{1,0:T(8,128)(2,1)S(1)} custom-call(s32[16,1]{1,0:T(8,128)S(1)} %copy.26.offset_ref, bf16[1,16,128,128]{3,2,1,0:T(8,128)(2,1)S(1)} %collective-permute-done.low_state, bf16[1,16,128,128]{3,2,1,0:T(8,128)(2,1)S(1)} %copy-done.1, bf16[1,16,128,128]{3,2,1,0:T(8,128)(2,1)S(1)} %collective-permute-done.1.high_state, ...), custom_call_target="tpu_custom_call" | custom-call | tf_op jit(solution)/shard_map/pallas_call | solution.py:125
  31.6 0.0 copy-start.7
  31.6 0.0 copy-start.10
  31.6 0.0 copy-start.8
  31.6 5.2 %multiply_reduce_fusion = (f32[48]{0:T(128)S(1)}, f32[48,2048]{1,0:T(8,128)S(1)}) fusion(bf16[48,2048]{1,0:T(8,128)(2,1)S(1)} %shard_map.181, bf16[2048,2048]{1,0:T(8,128)(2,1)} %param.31, bf16[48,2048]{1,0:T(8,128)(2,1)} %bitcast.23), kind=kOutput, calls=%fused_computation.20 | convolution fusion | flops 403046336 | bytes 9175232 | tf_op jit(solution)/shard_map/dot_general | solution.py:135
  36.8 0.0 copy-done.7
  36.8 0.1 multiply_convert_fusion.1
  36.9 0.0 copy-done.10
  36.9 0.3 fusion.26
  37.2 0.1 fusion.22
  37.4 0.8 concatenate.6
  38.1 0.0 all-gather.2.cloned.1.call-update
  38.2 0.0 reduce-scatter.2.cloned.1.call-start
  38.2 83.0 %all-gather.2.cloned.1.call-done = bf16[1536,2176]{1,0:T(8,128)(2,1)} async-done(((bf16[48,2176]{1,0:T(8,128)(2,1)}), bf16[1536,2176]{1,0:T(8,128)(2,1)}) %all-gather.2.cloned.1.call-update) | async-done | bytes 6684688 | tf_op jit(solution)/shard_map/all_gather | solution.py:155
  121.2 1.2 select_reduce_fusion
  122.4 0.0 copy-done.8
  122.4 0.0 copy-start.9
  122.4 5.8 %fusion.2 = f32[1536,256]{1,0:T(8,128)} fusion(bf16[1536,2176]{1,0:T(8,128)(2,1)} %all-gather.2.cloned.1.call-done, bf16[1,2048,256]{2,1,0:T(8,128)(2,1)S(1)} %copy-done.8), kind=kOutput, calls=%fused_computation.3 | convolution fusion | flops 1610612736 | bytes 8912896 | tf_op jit(solution)/shard_map/dot_general | solution.py:162
  128.2 0.0 copy-done
  128.2 0.0 copy-done.9
  128.2 10.5 %multiply_convert_fusion = bf16[1536,2048]{1,0:T(8,128)(2,1)} fusion(f32[1536]{0:T(1024)S(1)} %select_reduce_fusion, bf16[1536,2176]{1,0:T(8,128)(2,1)} %all-gather.2.cloned.1.call-done, f32[1536,256]{1,0:T(8,128)} %fusion.2, bf16[1,256,2048]{2,1,0:T(8,128)(2,1)S(1)} %copy-done, bf16[1,2048,256]{2,1,0:T(8,128)(2,1)S(1)} %copy-done.9), kind=kOutput, calls=%fused_computation | convolution fusion | flops 3229876224 | bytes 16259072 | tf_op jit(solution)/shard_map/dot_general | solution.py:164
  138.7 0.0 reduce-scatter.2.cloned.1.call-update
  138.7 113.0 %reduce-scatter.2.cloned.1.call-done = bf16[48,2048]{1,0:T(8,128)(2,1)} async-done(((bf16[1536,2048]{1,0:T(8,128)(2,1)}), bf16[48,2048]{1,0:T(8,128)(2,1)}) %reduce-scatter.2.cloned.1.call-update) | async-done | bytes 196624 | tf_op jit(solution)/shard_map/reduce_scatter | solution.py:168
  251.7 1.6 add_convert_fusion
  (8 shorter events, 0.1 us)
Async XLA Ops:
  6.5 121.7 %copy-start = (bf16[1,256,2048]{2,1,0:T(8,128)(2,1)S(1)}, bf16[1,256,2048]{2,1,0:T(8,128)(2,1)}, u32[]{:S(2)}) copy-start(bf16[1,256,2048]{2,1,0:T(8,128)(2,1)} %param.36) | copy-start | bytes 3145732
  6.5 114.7 %all-gather.2.cloned.1.call-start = ((), (), s32[]{:S(2)}) async-start(), calls=%async_computation.1 | async-start | bytes 6893568 | tf_op jit(solution)/shard_map/all_gather | solution.py:155
  6.5 13.4 %collective-permute-start.2 = (bf16[1,3,4096]{2,1,0:T(4,128)(2,1)}, bf16[1,3,4096]{2,1,0:T(4,128)(2,1)S(1)}, u32[]{:S(2)}, u32[]{:S(2)}) collective-permute-start(bf16[1,3,4096]{2,1,0:T(4,128)(2,1)} %own_conv.1), channel_id=1, source_target_pairs={{0,1},{1,2},{2,3},{3,4},{4,5},{5,6},{6,7},{7,8},{8,9},{9,10},{10,1... | collective-permute-start | bytes 73736 | tf_op jit(solution)/shard_map/ppermute | solution.py:117
  9.0 10.9 %collective-permute-start.3 = (bf16[1,3,4096]{2,1,0:T(4,128)(2,1)}, bf16[1,3,4096]{2,1,0:T(4,128)(2,1)S(1)}, u32[]{:S(2)}, u32[]{:S(2)}) collective-permute-start(bf16[1,3,4096]{2,1,0:T(4,128)(2,1)} %own_conv.1), channel_id=1, source_target_pairs={{1,0},{2,1},{3,2},{4,3},{5,4},{6,5},{7,6},{8,7},{9,8},{10,9},{11,1... | collective-permute-start | bytes 73736 | tf_op jit(solution)/shard_map/ppermute | solution.py:118
  10.3 9.7 %collective-permute-start = (bf16[1,16,128,128]{3,2,1,0:T(8,128)(2,1)}, bf16[1,16,128,128]{3,2,1,0:T(8,128)(2,1)S(1)}, u32[]{:S(2)}, u32[]{:S(2)}) collective-permute-start(bf16[1,16,128,128]{3,2,1,0:T(8,128)(2,1)} %own_state.1), channel_id=1, source_target_pairs={{0,1},{1,2},{2,3},{3,4},{4,5},{5,6},{6,7},{7,8},{8,9},{9,10},{10,1... | collective-permute-start | bytes 1572872 | tf_op jit(solution)/shard_map/ppermute | solution.py:119
  15.5 5.2 %collective-permute-start.1 = (bf16[1,16,128,128]{3,2,1,0:T(8,128)(2,1)}, bf16[1,16,128,128]{3,2,1,0:T(8,128)(2,1)S(1)}, u32[]{:S(2)}, u32[]{:S(2)}) collective-permute-start(bf16[1,16,128,128]{3,2,1,0:T(8,128)(2,1)} %own_state.1), channel_id=1, source_target_pairs={{1,0},{2,1},{3,2},{4,3},{5,4},{6,5},{7,6},{8,7},{9,8},{10,9},{11,1... | collective-permute-start | bytes 1572872 | tf_op jit(solution)/shard_map/ppermute | solution.py:120
  20.7 1.0 copy-start.1
  21.8 1.0 copy-start.2
  22.8 0.9 copy-start.3
  23.7 0.8 copy-start.4
  24.5 0.8 copy-start.5
  25.3 0.7 copy-start.6
  31.6 5.2 %copy-start.7 = (f32[2048]{0:T(1024)S(1)}, f32[2048]{0:T(1024)}, u32[]{:S(2)}) copy-start(f32[2048]{0:T(1024)} %param.32) | copy-start | bytes 24580
  31.6 5.3 %copy-start.10 = (bf16[2048,32]{0,1:T(8,128)(2,1)S(1)}, bf16[2048,32]{0,1:T(8,128)(2,1)}, u32[]{:S(2)}) copy-start(bf16[2048,32]{0,1:T(8,128)(2,1)} %param.33) | copy-start | bytes 393220
  31.6 90.8 %copy-start.8 = (bf16[1,2048,256]{2,1,0:T(8,128)(2,1)S(1)}, bf16[1,2048,256]{2,1,0:T(8,128)(2,1)}, u32[]{:S(2)}) copy-start(bf16[1,2048,256]{2,1,0:T(8,128)(2,1)} %param.34) | copy-start | bytes 3145732
  38.2 213.6 %reduce-scatter.2.cloned.1.call-start = ((), (), s32[]{:S(2)}) async-start(), calls=%async_computation.2 | async-start | bytes 6488064 | tf_op jit(solution)/shard_map/reduce_scatter | solution.py:168
  122.4 5.8 %copy-start.9 = (bf16[1,2048,256]{2,1,0:T(8,128)(2,1)S(1)}, bf16[1,2048,256]{2,1,0:T(8,128)(2,1)}, u32[]{:S(2)}) copy-start(bf16[1,2048,256]{2,1,0:T(8,128)(2,1)} %param.35) | copy-start | bytes 3145732
Sparse Core Ops, SparseCore 0:
  38.3 82.8 all-gather.1
  138.8 112.8 reduce-scatter.1

commit v2 on v1

--- a/solution.py
+++ b/solution.py
@@ -1,3 +1,4 @@
+import functools
 import math
 
 import jax
@@ -103,6 +104,209 @@
                 out_ref[t * slots : (t + 1) * slots, columns] = readout.astype(out_ref.dtype)
 
 
+GATHER_ORDERS = (("z", "x", "y"), ("z", "y", "x"), ("y", "z", "x"))
+
+
+class Place:
+    def __init__(self, count):
+        self.depth = count // 8
+        self.me = lax.axis_index("dev")
+        self.core = self.me % 2
+        self.own = {"x": (self.me // 2) % 2, "y": (self.me // 4) % 2, "z": self.me // 8}
+        self.sibling = self.me + 1 - 2 * self.core
+
+    def partners(self, axis):
+        if axis == "x":
+            return [(self.me + 2 - 4 * self.own["x"], 1 - self.own["x"], 1 - self.own["x"])]
+        if axis == "y":
+            return [(self.me + 4 - 8 * self.own["y"], 1 - self.own["y"], 1 - self.own["y"])]
+        found = []
+        for k in range(1, self.depth):
+            target = (self.own["z"] + k) % self.depth
+            source = (self.own["z"] + self.depth - k) % self.depth
+            found.append((target * 8 + self.me % 8, target, source))
+        return found
+
+    def meet(self):
+        barrier = pltpu.get_barrier_semaphore()
+        others = [self.sibling] + [p[0] for a in ("x", "y", "z") for p in self.partners(a)]
+        for other in others:
+            pl.semaphore_signal(
+                barrier, inc=1, device_id={"dev": other}, device_id_type=pl.DeviceIdType.MESH
+            )
+        pl.semaphore_wait(barrier, len(others))
+
+
+LANES = {"x": 0, "y": 1, "core": 2, "z": 3}
+
+
+def remote(source, target, send, receive, device):
+    return pltpu.make_async_remote_copy(
+        src_ref=source, dst_ref=target, send_sem=send, recv_sem=receive,
+        device_id={"dev": device}, device_id_type=pl.DeviceIdType.MESH,
+    )
+
+
+def gather_kernel(count, in_ref, out_ref, local_sem, send_sem, recv_sem):
+    steps = in_ref.shape[0]
+    place = Place(count)
+    own = place.own
+    local = []
+    for t in range(steps):
+        copy = pltpu.make_async_copy(
+            in_ref.at[t], out_ref.at[t, own["z"], own["y"], own["x"], place.core], local_sem.at[t]
+        )
+        copy.start()
+        local.append(copy)
+    place.meet()
+    sent = []
+    arriving = [[] for _ in range(steps)]
+    for stage in range(3):
+        for t in range(steps):
+            order = GATHER_ORDERS[t % 3]
+            if stage == 0:
+                local[t].wait()
+            for copy in arriving[t]:
+                copy.wait_recv()
+            arriving[t] = []
+            axis = order[stage]
+            done = order[:stage]
+
+            def region(position):
+                at = [slice(None) if a in done else own[a] for a in ("z", "y", "x")]
+                at[("z", "y", "x").index(axis)] = position
+                return out_ref.at[t, at[0], at[1], at[2], place.core]
+
+            for k, (device, _, source) in enumerate(place.partners(axis)):
+                lane = LANES[axis] + k
+                copy = remote(
+                    region(own[axis]), region(own[axis]), send_sem.at[t, lane],
+                    recv_sem.at[t, lane], device,
+                )
+                copy.start()
+                sent.append(copy)
+                arriving[t].append(
+                    remote(
+                        region(source), region(source), send_sem.at[t, lane],
+                        recv_sem.at[t, lane], device,
+                    )
+                )
+    last = []
+    for t in range(steps):
+        for copy in arriving[t]:
+            copy.wait_recv()
+        plane = out_ref.at[t, :, :, :, place.core]
+        other = out_ref.at[t, :, :, :, 1 - place.core]
+        sems = (send_sem.at[t, LANES["core"]], recv_sem.at[t, LANES["core"]], place.sibling)
+        copy = remote(plane, plane, *sems)
+        copy.start()
+        sent.append(copy)
+        last.append(remote(other, other, *sems))
+    for copy in last:
+        copy.wait_recv()
+    for copy in sent:
+        copy.wait_send()
+
+
+def scatter_kernel(
+    count, in_ref, out_ref, total, from_core, from_x, from_y, from_z, send_sem, recv_sem
+):
+    steps = in_ref.shape[0]
+    place = Place(count)
+    own = place.own
+    place.meet()
+    sent = []
+    arriving = []
+    for t in range(steps):
+        copy = remote(
+            in_ref.at[t, :, :, :, 1 - place.core], from_core.at[t],
+            send_sem.at[t, LANES["core"]], recv_sem.at[t, LANES["core"]], place.sibling,
+        )
+        copy.start()
+        sent.append(copy)
+        arriving.append([copy])
+    landed = [None] * steps
+    for stage in range(4):
+        for t in range(steps):
+            order = GATHER_ORDERS[t % 3][::-1]
+            for copy in arriving[t]:
+                copy.wait_recv()
+            arriving[t] = []
+            done = order[:stage]
+            at = [own[a] if a in done else slice(None) for a in ("z", "y", "x")]
+            if stage == 0:
+                value = in_ref[t, :, :, :, place.core].astype(jnp.float32)
+                value = value + from_core[t].astype(jnp.float32)
+            else:
+                value = total[t, at[0], at[1], at[2]].astype(jnp.float32)
+                for ref, index in landed[t]:
+                    value = value + ref[index].astype(jnp.float32)
+            if stage == 3:
+                out_ref[t] = value
+                continue
+            total[t, at[0], at[1], at[2]] = value.astype(total.dtype)
+            axis = order[stage]
+            landed[t] = []
+            for k, (device, target, _) in enumerate(place.partners(axis)):
+                spot = dict(zip(("z", "y", "x"), at))
+                source = dict(spot)
+                source[axis] = target
+                if axis == "x":
+                    buffer, index = from_x, (t, spot["z"], spot["y"])
+                elif axis == "y":
+                    buffer, index = from_y, (t, spot["z"], spot["x"])
+                else:
+                    buffer, index = from_z, (t, k, spot["y"], spot["x"])
+                lane = LANES[axis] + k
+                copy = remote(
+                    total.at[t, source["z"], source["y"], source["x"]], buffer.at[index],
+                    send_sem.at[t, lane], recv_sem.at[t, lane], device,
+                )
+                copy.start()
+                sent.append(copy)
+                arriving[t].append(copy)
+                landed[t].append((buffer, index))
+    for copy in sent:
+        copy.wait_send()
+
+
+def gathered_rows(rows, count):
+    steps, slots, width = rows.shape
+    depth = count // 8
+    sems = pltpu.SemaphoreType.DMA((steps, 2 + depth))
+    return pl.pallas_call(
+        functools.partial(gather_kernel, count),
+        out_shape=jax.ShapeDtypeStruct((steps, depth, 2, 2, 2, slots, width), rows.dtype),
+        in_specs=[pl.BlockSpec(memory_space=pl.ANY)],
+        out_specs=pl.BlockSpec(memory_space=pl.ANY),
+        scratch_shapes=[pltpu.SemaphoreType.DMA((steps,)), sems, sems],
+        compiler_params=pltpu.CompilerParams(collective_id=0, has_side_effects=True),
+    )(rows)
+
+
+def scattered_sum(parts, count):
+    steps, depth, _, _, _, slots, width = parts.shape
+    sems = pltpu.SemaphoreType.DMA((steps, 2 + depth))
+    return pl.pallas_call(
+        functools.partial(scatter_kernel, count),
+        out_shape=jax.ShapeDtypeStruct((steps, slots, width), jnp.float32),
+        in_specs=[pl.BlockSpec(memory_space=pltpu.VMEM)],
+        out_specs=pl.BlockSpec(memory_space=pltpu.VMEM),
+        scratch_shapes=[
+            pltpu.VMEM((steps, depth, 2, 2, slots, width), parts.dtype),
+            pltpu.VMEM((steps, depth, 2, 2, slots, width), parts.dtype),
+            pltpu.VMEM((steps, depth, 2, slots, width), parts.dtype),
+            pltpu.VMEM((steps, depth, 2, slots, width), parts.dtype),
+            pltpu.VMEM((steps, depth - 1, 2, 2, slots, width), parts.dtype),
+            sems,
+            sems,
+        ],
+        compiler_params=pltpu.CompilerParams(
+            collective_id=1, has_side_effects=True, vmem_limit_bytes=56 * 1024 * 1024
+        ),
+    )(parts)
+
+
 def body(
     prompt_state, conv_state, slot_prompt, mixed_input, output_gate, residual, beta_logit,
     decay_logit, decay_base, decay_bias, head_gain, conv_weight, out_weight, post_gain, router,
@@ -152,7 +356,8 @@
     tail = jnp.concatenate(
         [high, low, jnp.zeros((rows, extra - 2 * experts), jnp.float32)], axis=1
     ).astype(jnp.bfloat16)
-    gathered = lax.all_gather(jnp.concatenate([normed, tail], axis=1), "dev", axis=0, tiled=True)
+    sending = jnp.concatenate([normed, tail], axis=1).reshape(steps, slots, width + extra)
+    gathered = gathered_rows(sending, count).reshape(steps * count * slots, width + extra)
     tokens = gathered[:, :width]
     column = jnp.arange(extra, dtype=jnp.int32)
     mine = (column == me) | (column == me + experts)
@@ -165,8 +370,9 @@
         hidden.astype(jnp.bfloat16), expert_down[0], preferred_element_type=jnp.float32
     )
     result = (result * weight).astype(jnp.bfloat16)
-    mixture = lax.psum_scatter(result, "dev", scatter_dimension=0, tiled=True)
-    layer_out = (carried + mixture.astype(jnp.float32)).astype(jnp.bfloat16)
+    result = result.reshape(steps, count // 8, 2, 2, 2, slots, width)
+    mixture = scattered_sum(result, count).reshape(rows, width)
+    layer_out = (carried + mixture).astype(jnp.bfloat16)
     return layer_out.reshape(steps, slots, width)
 
 

time: 261 us -> 175 us (0.67)
  waiting for transfers between devices: 197 us -> 0.73 us
  Pallas kernels: 5.63 us -> 129 us
  between operations: 13.6 us -> 0.19 us
    pallas_call x0 -> x2, Pallas kernels: none -> 123 us  [the longest x1 65.2 us: gathered_rows(): pl.pallas_call(functools.partial(gather_kernel, count), out_shape=jax.Sha...]
    reduce_scatter x1 -> x0, waiting for transfers between devices: 113 us -> none  [body(): mixture = lax.psum_scatter(result, 'dev', scatter_dimension=0, tiled=True)]
    all_gather x1 -> x0, waiting for transfers between devices: 83 us -> none  [body(): lax.all_gather(jnp.concatenate([normed, tail], axis=1), 'dev', axis=0, ti...]
  transfers between devices with their start and end apart: 6 -> 4, of which waited for: 3 -> 1; matrix products, arithmetic and copies ran while one was open for 1% -> 2% of each run, Pallas kernels for 0% -> 0%
where the time goes in v2:
time: 175 us; the launch traced here: 174 us
  Pallas kernels  129 us (74%)
  matrix products  21.7 us (12%)
  starting transfers between devices  10.2 us (6%)
  local copies, waits for them, and re-layouts  7.01 us (4%)
  other arithmetic  5.27 us (3%)
    pallas_call x1, Pallas kernels, gathered_rows(): pl.pallas_call(functools.partial(gather_kernel, count), out_shape=jax.Sha...  65.2 us
    pallas_call x1, Pallas kernels, scattered_sum(): pl.pallas_call(functools.partial(scatter_kernel, count), out_shape=jax.Sh...  58.2 us
    dot_general x1, matrix products, body(): jnp.dot(hidden.astype(jnp.bfloat16), expert_down[0], preferred_element_ty...  10.4 us
    dot_general x1, matrix products, body(): jnp.dot(tokens, expert_gate[0], preferred_element_type=jnp.float32)  5.83 us
    pallas_call x1, Pallas kernels, body(): pl.pallas_call(delta_kernel, out_shape=jax.ShapeDtypeStruct((rows, heads...  5.66 us
    unnamed x22, local copies, waits for them, and re-layouts  5.24 us
    ppermute x1, starting transfers between devices, body(): low_state = lax.ppermute(prompt_state, 'dev', forward)  5.17 us
    dot_general x1, matrix products, body(): jnp.dot(gated, out_weight, preferred_element_type=jnp.float32)  5.12 us
  transfers between devices with their start and end apart: 4, of which 1 were waited for; matrix products, arithmetic and copies ran while one was open for 2% of the time, Pallas kernels for 0%

profile of v2, /device:TPU:0, one launch (start us, length us, event | category | flops | bytes accessed | tf_op | source)
XLA Modules:
  0.0 174.2 jit_solution(1142095336200829148)
XLA Ops:
  0.0 0.0 copy-start
  0.0 2.5 %collective-permute-start.2 = (bf16[1,3,4096]{2,1,0:T(4,128)(2,1)}, bf16[1,3,4096]{2,1,0:T(4,128)(2,1)S(1)}, u32[]{:S(2)}, u32[]{:S(2)}) collective-permute-start(bf16[1,3,4096]{2,1,0:T(4,128)(2,1)} %own_conv.1), channel_id=1, source_target_pairs={{0,1},{1,2},{2,3},{3,4},{4,5},{5,6},{6,7},{7,8},{8,9},{9,10},{10,1... | collective-permute-start | bytes 73736 | tf_op jit(solution)/shard_map/ppermute | solution.py:321
  2.5 1.3 collective-permute-start.3
  3.8 5.2 %collective-permute-start = (bf16[1,16,128,128]{3,2,1,0:T(8,128)(2,1)}, bf16[1,16,128,128]{3,2,1,0:T(8,128)(2,1)S(1)}, u32[]{:S(2)}, u32[]{:S(2)}) collective-permute-start(bf16[1,16,128,128]{3,2,1,0:T(8,128)(2,1)} %own_state.1), channel_id=1, source_target_pairs={{0,1},{1,2},{2,3},{3,4},{4,5},{5,6},{6,7},{7,8},{8,9},{9,10},{10,1... | collective-permute-start | bytes 1572872 | tf_op jit(solution)/shard_map/ppermute | solution.py:323
  9.0 1.3 collective-permute-start.1
  10.3 0.7 exponential_negate_fusion
  10.9 0.8 eq.27
  11.8 0.7 subtract_bitcast_fusion
  12.4 0.8 fusion.25
  13.3 0.1 copy.26.offset_ref
  13.4 0.1 copy.28
  13.4 0.0 collective-permute-done.2.low_conv
  13.5 0.0 collective-permute-done.3.high_conv
  13.5 0.0 collective-permute-done.low_state
  13.5 0.7 collective-permute-done.1.high_state
  14.2 0.0 copy-start.1
  14.2 1.0 copy-done.1
  15.2 0.0 copy-start.2
  15.2 1.0 copy-done.2
  16.2 0.0 copy-start.3
  16.2 0.9 copy-done.3
  17.2 0.0 copy-start.4
  17.2 0.8 copy-done.4
  18.0 0.0 copy-start.5
  18.0 0.8 copy-done.5
  18.8 0.0 copy-start.6
  18.8 0.7 copy-done.6
  19.4 5.7 %shard_map.181 = bf16[48,2048]{1,0:T(8,128)(2,1)S(1)} custom-call(s32[16,1]{1,0:T(8,128)S(1)} %copy.26.offset_ref, bf16[1,16,128,128]{3,2,1,0:T(8,128)(2,1)S(1)} %collective-permute-done.low_state, bf16[1,16,128,128]{3,2,1,0:T(8,128)(2,1)S(1)} %copy-done.1, bf16[1,16,128,128]{3,2,1,0:T(8,128)(2,1)S(1)} %collective-permute-done.1.high_state, ...), custom_call_target="tpu_custom_call" | custom-call | tf_op jit(solution)/shard_map/pallas_call | solution.py:329
  25.1 0.0 copy-start.7
  25.1 0.0 copy-start.10
  25.1 5.1 %multiply_reduce_fusion = (f32[48]{0:T(128)S(1)}, f32[48,2048]{1,0:T(8,128)S(1)}) fusion(bf16[48,2048]{1,0:T(8,128)(2,1)S(1)} %shard_map.181, bf16[2048,2048]{1,0:T(8,128)(2,1)} %param.31, bf16[48,2048]{1,0:T(8,128)(2,1)} %bitcast.35), kind=kOutput, calls=%fused_computation.21 | convolution fusion | flops 403046336 | bytes 9175232 | tf_op jit(solution)/shard_map/dot_general | solution.py:339
  30.2 0.0 copy-start.8
  30.3 0.0 copy-done.7
  30.3 0.1 multiply_convert_fusion.1
  30.4 0.0 copy-done.10
  30.4 0.3 fusion.27
  30.7 0.1 fusion.23
  30.8 0.8 concatenate.6
  31.6 65.2 %shard_map.182 = bf16[3,4,2,2,2,16,2176]{6,5,4,3,2,1,0:T(8,128)(2,1)} custom-call(bf16[3,16,2176]{2,1,0:T(8,128)(2,1)} %bitcast.34), custom_call_target="tpu_custom_call" | custom-call | tf_op jit(solution)/shard_map/pallas_call | solution.py:277
  96.8 1.2 select_reduce_fusion
  97.9 0.0 copy-done.8
  98.0 0.0 copy-start.9
  98.0 5.8 %fusion.2 = f32[1536,256]{1,0:T(8,128)} fusion(bf16[1536,2176]{1,0:T(8,128)(2,1)} %bitcast.31, bf16[1,2048,256]{2,1,0:T(8,128)(2,1)S(1)} %copy-done.8), kind=kOutput, calls=%fused_computation.3 | convolution fusion | flops 1610612736 | bytes 8912896 | tf_op jit(solution)/shard_map/dot_general | solution.py:367
  103.8 0.0 copy-done
  103.8 0.0 copy-done.9
  103.8 10.4 %multiply_convert_fusion = bf16[1536,2048]{1,0:T(8,128)(2,1)} fusion(f32[1536]{0:T(1024)S(1)} %select_reduce_fusion, bf16[1536,2176]{1,0:T(8,128)(2,1)} %bitcast.32, f32[1536,256]{1,0:T(8,128)} %fusion.2, bf16[1,256,2048]{2,1,0:T(8,128)(2,1)S(1)} %copy-done, bf16[1,2048,256]{2,1,0:T(8,128)(2,1)S(1)} %copy-done.9), kind=kOutput, calls=%fused_computation | convolution fusion | flops 3229876224 | bytes 16259072 | tf_op jit(solution)/shard_map/dot_general | solution.py:369
  114.2 58.2 %shard_map.183 = f32[3,16,2048]{2,1,0:T(8,128)} custom-call(bf16[3,4,2,2,2,16,2048]{6,5,4,3,2,1,0:T(8,128)(2,1)} %bitcast.33), custom_call_target="tpu_custom_call" | custom-call | tf_op jit(solution)/shard_map/pallas_call | solution.py:290
  172.5 1.7 fusion.21
  (4 shorter events, 0.1 us)
Async XLA Ops:
  0.0 103.8 %copy-start = (bf16[1,256,2048]{2,1,0:T(8,128)(2,1)S(1)}, bf16[1,256,2048]{2,1,0:T(8,128)(2,1)}, u32[]{:S(2)}) copy-start(bf16[1,256,2048]{2,1,0:T(8,128)(2,1)} %param.36) | copy-start | bytes 3145732
  0.0 13.4 %collective-permute-start.2 = (bf16[1,3,4096]{2,1,0:T(4,128)(2,1)}, bf16[1,3,4096]{2,1,0:T(4,128)(2,1)S(1)}, u32[]{:S(2)}, u32[]{:S(2)}) collective-permute-start(bf16[1,3,4096]{2,1,0:T(4,128)(2,1)} %own_conv.1), channel_id=1, source_target_pairs={{0,1},{1,2},{2,3},{3,4},{4,5},{5,6},{6,7},{7,8},{8,9},{9,10},{10,1... | collective-permute-start | bytes 73736 | tf_op jit(solution)/shard_map/ppermute | solution.py:321
  2.5 11.0 %collective-permute-start.3 = (bf16[1,3,4096]{2,1,0:T(4,128)(2,1)}, bf16[1,3,4096]{2,1,0:T(4,128)(2,1)S(1)}, u32[]{:S(2)}, u32[]{:S(2)}) collective-permute-start(bf16[1,3,4096]{2,1,0:T(4,128)(2,1)} %own_conv.1), channel_id=1, source_target_pairs={{1,0},{2,1},{3,2},{4,3},{5,4},{6,5},{7,6},{8,7},{9,8},{10,9},{11,1... | collective-permute-start | bytes 73736 | tf_op jit(solution)/shard_map/ppermute | solution.py:322
  3.8 9.7 %collective-permute-start = (bf16[1,16,128,128]{3,2,1,0:T(8,128)(2,1)}, bf16[1,16,128,128]{3,2,1,0:T(8,128)(2,1)S(1)}, u32[]{:S(2)}, u32[]{:S(2)}) collective-permute-start(bf16[1,16,128,128]{3,2,1,0:T(8,128)(2,1)} %own_state.1), channel_id=1, source_target_pairs={{0,1},{1,2},{2,3},{3,4},{4,5},{5,6},{6,7},{7,8},{8,9},{9,10},{10,1... | collective-permute-start | bytes 1572872 | tf_op jit(solution)/shard_map/ppermute | solution.py:323
  9.0 5.2 %collective-permute-start.1 = (bf16[1,16,128,128]{3,2,1,0:T(8,128)(2,1)}, bf16[1,16,128,128]{3,2,1,0:T(8,128)(2,1)S(1)}, u32[]{:S(2)}, u32[]{:S(2)}) collective-permute-start(bf16[1,16,128,128]{3,2,1,0:T(8,128)(2,1)} %own_state.1), channel_id=1, source_target_pairs={{1,0},{2,1},{3,2},{4,3},{5,4},{6,5},{7,6},{8,7},{9,8},{10,9},{11,1... | collective-permute-start | bytes 1572872 | tf_op jit(solution)/shard_map/ppermute | solution.py:324
  14.2 1.0 copy-start.1
  15.2 1.0 copy-start.2
  16.2 0.9 copy-start.3
  17.2 0.8 copy-start.4
  18.0 0.8 copy-start.5
  18.8 0.7 copy-start.6
  25.1 5.2 %copy-start.7 = (f32[2048]{0:T(1024)S(1)}, f32[2048]{0:T(1024)}, u32[]{:S(2)}) copy-start(f32[2048]{0:T(1024)} %param.32) | copy-start | bytes 24580
  25.1 5.3 %copy-start.10 = (bf16[2048,32]{0,1:T(8,128)(2,1)S(1)}, bf16[2048,32]{0,1:T(8,128)(2,1)}, u32[]{:S(2)}) copy-start(bf16[2048,32]{0,1:T(8,128)(2,1)} %param.33) | copy-start | bytes 393220
  30.2 67.7 %copy-start.8 = (bf16[1,2048,256]{2,1,0:T(8,128)(2,1)S(1)}, bf16[1,2048,256]{2,1,0:T(8,128)(2,1)}, u32[]{:S(2)}) copy-start(bf16[1,2048,256]{2,1,0:T(8,128)(2,1)} %param.34) | copy-start | bytes 3145732
  98.0 5.8 %copy-start.9 = (bf16[1,2048,256]{2,1,0:T(8,128)(2,1)S(1)}, bf16[1,2048,256]{2,1,0:T(8,128)(2,1)}, u32[]{:S(2)}) copy-start(bf16[1,2048,256]{2,1,0:T(8,128)(2,1)} %param.35) | copy-start | bytes 3145732

commit v3 on v2

--- a/solution.py
+++ b/solution.py
@@ -147,7 +147,10 @@
     )
 
 
-def gather_kernel(count, in_ref, out_ref, local_sem, send_sem, recv_sem):
+def routed_kernel(
+    count, in_ref, gate_ref, up_ref, down_ref, mixture_ref, out_ref, result, fetched, total,
+    from_core, from_x, from_y, from_z, local_sem, send_sem, recv_sem, back_send, back_recv,
+):
     steps = in_ref.shape[0]
     place = Place(count)
     own = place.own
@@ -191,7 +194,79 @@
                         recv_sem.at[t, lane], device,
                     )
                 )
-    last = []
+
+    width = down_ref.shape[1]
+    slots, full = in_ref.shape[1:]
+    batch = 16 * slots
+    experts = count
+
+    def compute(t):
+        copy = pltpu.make_async_copy(out_ref.at[t], fetched, local_sem.at[steps])
+        copy.start()
+        copy.wait()
+
+        def part(i, carry):
+            span = pl.ds(2 * i, 2)
+            rows = fetched[span].reshape(batch, full)
+            tokens, tail = rows[:, :width], rows[:, width:].astype(jnp.float32)
+            column = lax.broadcasted_iota(jnp.int32, tail.shape, 1)
+            mine = (column == place.me) | (column == place.me + experts)
+            weight = jnp.sum(jnp.where(mine, tail, 0.0), axis=1, keepdims=True)
+            hidden = jnp.dot(tokens, gate_ref[...], preferred_element_type=jnp.float32)
+            hidden = hidden * jax.nn.sigmoid(hidden)
+            hidden = hidden * jnp.dot(tokens, up_ref[...], preferred_element_type=jnp.float32)
+            value = jnp.dot(
+                hidden.astype(jnp.bfloat16), down_ref[...], preferred_element_type=jnp.float32
+            )
+            value = (value * weight).astype(result.dtype)
+            result[t, span] = value.reshape(2, 2, 2, 2, slots, width)
+            return carry
+
+        lax.fori_loop(0, place.depth // 2, part, 0)
+
+    incoming = [[] for _ in range(steps)]
+    landed = [None] * steps
+
+    def advance(stage, t):
+        order = GATHER_ORDERS[t % 3][::-1]
+        for copy in incoming[t]:
+            copy.wait_recv()
+        incoming[t] = []
+        done = order[:stage]
+        at = [own[a] if a in done else slice(None) for a in ("z", "y", "x")]
+        if stage == 0:
+            value = result[t, :, :, :, place.core].astype(jnp.float32)
+            value = value + from_core[t].astype(jnp.float32)
+        else:
+            value = total[t, at[0], at[1], at[2]].astype(jnp.float32)
+            for ref, index in landed[t]:
+                value = value + ref[index].astype(jnp.float32)
+        if stage == 3:
+            mixture_ref[t] = value
+            return
+        total[t, at[0], at[1], at[2]] = value.astype(total.dtype)
+        axis = order[stage]
+        landed[t] = []
+        for k, (device, target, _) in enumerate(place.partners(axis)):
+            spot = dict(zip(("z", "y", "x"), at))
+            source = dict(spot)
+            source[axis] = target
+            if axis == "x":
+                buffer, index = from_x, (t, spot["z"], spot["y"])
+            elif axis == "y":
+                buffer, index = from_y, (t, spot["z"], spot["x"])
+            else:
+                buffer, index = from_z, (t, k, spot["y"], spot["x"])
+            lane = LANES[axis] + k
+            copy = remote(
+                total.at[t, source["z"], source["y"], source["x"]], buffer.at[index],
+                back_send.at[t, lane], back_recv.at[t, lane], device,
+            )
+            copy.start()
+            sent.append(copy)
+            incoming[t].append(copy)
+            landed[t].append((buffer, index))
+
     for t in range(steps):
         for copy in arriving[t]:
             copy.wait_recv()
@@ -201,110 +276,57 @@
         copy = remote(plane, plane, *sems)
         copy.start()
         sent.append(copy)
-        last.append(remote(other, other, *sems))
-    for copy in last:
-        copy.wait_recv()
-    for copy in sent:
-        copy.wait_send()
-
-
-def scatter_kernel(
-    count, in_ref, out_ref, total, from_core, from_x, from_y, from_z, send_sem, recv_sem
-):
-    steps = in_ref.shape[0]
-    place = Place(count)
-    own = place.own
-    place.meet()
-    sent = []
-    arriving = []
-    for t in range(steps):
+        remote(other, other, *sems).wait_recv()
+        compute(t)
         copy = remote(
-            in_ref.at[t, :, :, :, 1 - place.core], from_core.at[t],
-            send_sem.at[t, LANES["core"]], recv_sem.at[t, LANES["core"]], place.sibling,
+            result.at[t, :, :, :, 1 - place.core], from_core.at[t],
+            back_send.at[t, LANES["core"]], back_recv.at[t, LANES["core"]], place.sibling,
         )
         copy.start()
         sent.append(copy)
-        arriving.append([copy])
-    landed = [None] * steps
-    for stage in range(4):
+        incoming[t].append(copy)
+        if t > 0:
+            advance(0, t - 1)
+    advance(0, steps - 1)
+    for stage in range(1, 4):
         for t in range(steps):
-            order = GATHER_ORDERS[t % 3][::-1]
-            for copy in arriving[t]:
-                copy.wait_recv()
-            arriving[t] = []
-            done = order[:stage]
-            at = [own[a] if a in done else slice(None) for a in ("z", "y", "x")]
-            if stage == 0:
-                value = in_ref[t, :, :, :, place.core].astype(jnp.float32)
-                value = value + from_core[t].astype(jnp.float32)
-            else:
-                value = total[t, at[0], at[1], at[2]].astype(jnp.float32)
-                for ref, index in landed[t]:
-                    value = value + ref[index].astype(jnp.float32)
-            if stage == 3:
-                out_ref[t] = value
-                continue
-            total[t, at[0], at[1], at[2]] = value.astype(total.dtype)
-            axis = order[stage]
-            landed[t] = []
-            for k, (device, target, _) in enumerate(place.partners(axis)):
-                spot = dict(zip(("z", "y", "x"), at))
-                source = dict(spot)
-                source[axis] = target
-                if axis == "x":
-                    buffer, index = from_x, (t, spot["z"], spot["y"])
-                elif axis == "y":
-                    buffer, index = from_y, (t, spot["z"], spot["x"])
-                else:
-                    buffer, index = from_z, (t, k, spot["y"], spot["x"])
-                lane = LANES[axis] + k
-                copy = remote(
-                    total.at[t, source["z"], source["y"], source["x"]], buffer.at[index],
-                    send_sem.at[t, lane], recv_sem.at[t, lane], device,
-                )
-                copy.start()
-                sent.append(copy)
-                arriving[t].append(copy)
-                landed[t].append((buffer, index))
+            advance(stage, t)
     for copy in sent:
         copy.wait_send()
 
 
-def gathered_rows(rows, count):
-    steps, slots, width = rows.shape
+def routed_sum(rows, gate, up, down, count):
+    steps, slots, full = rows.shape
+    width = down.shape[1]
     depth = count // 8
     sems = pltpu.SemaphoreType.DMA((steps, 2 + depth))
+    whole = (depth, 2, 2, 2, slots)
+    kind = rows.dtype
+    vmem = pl.BlockSpec(memory_space=pltpu.VMEM)
+    hbm = pl.BlockSpec(memory_space=pl.ANY)
     return pl.pallas_call(
-        functools.partial(gather_kernel, count),
-        out_shape=jax.ShapeDtypeStruct((steps, depth, 2, 2, 2, slots, width), rows.dtype),
-        in_specs=[pl.BlockSpec(memory_space=pl.ANY)],
-        out_specs=pl.BlockSpec(memory_space=pl.ANY),
-        scratch_shapes=[pltpu.SemaphoreType.DMA((steps,)), sems, sems],
-        compiler_params=pltpu.CompilerParams(collective_id=0, has_side_effects=True),
-    )(rows)
-
-
-def scattered_sum(parts, count):
-    steps, depth, _, _, _, slots, width = parts.shape
-    sems = pltpu.SemaphoreType.DMA((steps, 2 + depth))
-    return pl.pallas_call(
-        functools.partial(scatter_kernel, count),
-        out_shape=jax.ShapeDtypeStruct((steps, slots, width), jnp.float32),
-        in_specs=[pl.BlockSpec(memory_space=pltpu.VMEM)],
-        out_specs=pl.BlockSpec(memory_space=pltpu.VMEM),
+        functools.partial(routed_kernel, count),
+        out_shape=(
+            jax.ShapeDtypeStruct((steps, slots, width), jnp.float32),
+            jax.ShapeDtypeStruct((steps,) + whole + (full,), kind),
+        ),
+        in_specs=[hbm, vmem, vmem, vmem],
+        out_specs=(vmem, hbm),
         scratch_shapes=[
-            pltpu.VMEM((steps, depth, 2, 2, slots, width), parts.dtype),
-            pltpu.VMEM((steps, depth, 2, 2, slots, width), parts.dtype),
-            pltpu.VMEM((steps, depth, 2, slots, width), parts.dtype),
-            pltpu.VMEM((steps, depth, 2, slots, width), parts.dtype),
-            pltpu.VMEM((steps, depth - 1, 2, 2, slots, width), parts.dtype),
-            sems,
-            sems,
+            pltpu.VMEM((steps,) + whole + (width,), kind),
+            pltpu.VMEM(whole + (full,), kind),
+            pltpu.VMEM((steps, depth, 2, 2, slots, width), kind),
+            pltpu.VMEM((steps, depth, 2, 2, slots, width), kind),
+            pltpu.VMEM((steps, depth, 2, slots, width), kind),
+            pltpu.VMEM((steps, depth, 2, slots, width), kind),
+            pltpu.VMEM((steps, depth - 1, 2, 2, slots, width), kind),
+            pltpu.SemaphoreType.DMA((steps + 1,)),
+            sems, sems, sems, sems,
         ],
         compiler_params=pltpu.CompilerParams(
-            collective_id=1, has_side_effects=True, vmem_limit_bytes=56 * 1024 * 1024
+            collective_id=0, has_side_effects=True, vmem_limit_bytes=58 * 1024 * 1024
         ),
-    )(parts)
+    )(rows, gate, up, down)[0]
 
 
 def body(
@@ -357,21 +379,8 @@
         [high, low, jnp.zeros((rows, extra - 2 * experts), jnp.float32)], axis=1
     ).astype(jnp.bfloat16)
     sending = jnp.concatenate([normed, tail], axis=1).reshape(steps, slots, width + extra)
-    gathered = gathered_rows(sending, count).reshape(steps * count * slots, width + extra)
-    tokens = gathered[:, :width]
-    column = jnp.arange(extra, dtype=jnp.int32)
-    mine = (column == me) | (column == me + experts)
-    weight = jnp.sum(
-        jnp.where(mine, gathered[:, width:].astype(jnp.float32), 0.0), axis=1, keepdims=True
-    )
-    hidden = jax.nn.silu(jnp.dot(tokens, expert_gate[0], preferred_element_type=jnp.float32))
-    hidden = hidden * jnp.dot(tokens, expert_up[0], preferred_element_type=jnp.float32)
-    result = jnp.dot(
-        hidden.astype(jnp.bfloat16), expert_down[0], preferred_element_type=jnp.float32
-    )
-    result = (result * weight).astype(jnp.bfloat16)
-    result = result.reshape(steps, count // 8, 2, 2, 2, slots, width)
-    mixture = scattered_sum(result, count).reshape(rows, width)
+    mixture = routed_sum(sending, expert_gate[0], expert_up[0], expert_down[0], count)
+    mixture = mixture.reshape(rows, width)
     layer_out = (carried + mixture).astype(jnp.bfloat16)
     return layer_out.reshape(steps, slots, width)
 

time: 175 us -> 157 us (0.90)
  matrix products: 21.7 us -> 5.38 us
    dot_general x2 -> x0, matrix products: 16.3 us -> none  [the longest x1 10.4 us: body(): jnp.dot(hidden.astype(jnp.bfloat16), expert_down[0], preferred_element_ty...]
    pallas_call x2 -> x1, Pallas kernels: 123 us -> 123 us  [routed_sum(): pl.pallas_call(functools.partial(routed_kernel, count), out_shape=(jax.Sh...]
    unnamed x22 -> x16, local copies, waits for them, and re-layouts: 5.24 us -> 5.22 us
where the time goes in v3:
time: 157 us; the launch traced here: 156 us
  Pallas kernels  129 us (82%)
  starting transfers between devices  10.2 us (6%)
  local copies, waits for them, and re-layouts  7 us (4%)
  matrix products  5.38 us (3%)
  other arithmetic  4.07 us (3%)
    pallas_call x1, Pallas kernels, routed_sum(): pl.pallas_call(functools.partial(routed_kernel, count), out_shape=(jax.Sh...  123 us
    pallas_call x1, Pallas kernels, body(): pl.pallas_call(delta_kernel, out_shape=jax.ShapeDtypeStruct((rows, heads...  5.61 us
    unnamed x16, local copies, waits for them, and re-layouts  5.22 us
    ppermute x1, starting transfers between devices, body(): low_state = lax.ppermute(prompt_state, 'dev', forward)  5.17 us
    dot_general x1, matrix products, body(): jnp.dot(gated, out_weight, preferred_element_type=jnp.float32)  5.07 us
  transfers between devices with their start and end apart: 4, of which 1 were waited for; matrix products, arithmetic and copies ran while one was open for 2% of the time, Pallas kernels for 0%

profile of v3, /device:TPU:0, one launch (start us, length us, event | category | flops | bytes accessed | tf_op | source)
XLA Modules:
  0.0 156.4 jit_solution(10752549783351349685)
XLA Ops:
  0.0 0.0 copy-start
  0.0 2.5 %collective-permute-start.2 = (bf16[1,3,4096]{2,1,0:T(4,128)(2,1)}, bf16[1,3,4096]{2,1,0:T(4,128)(2,1)S(1)}, u32[]{:S(2)}, u32[]{:S(2)}) collective-permute-start(bf16[1,3,4096]{2,1,0:T(4,128)(2,1)} %own_conv.1), channel_id=1, source_target_pairs={{0,1},{1,2},{2,3},{3,4},{4,5},{5,6},{6,7},{7,8},{8,9},{9,10},{10,1... | collective-permute-start | bytes 73736 | tf_op jit(solution)/shard_map/ppermute | solution.py:343
  2.5 1.3 collective-permute-start.3
  3.8 5.2 %collective-permute-start = (bf16[1,16,128,128]{3,2,1,0:T(8,128)(2,1)}, bf16[1,16,128,128]{3,2,1,0:T(8,128)(2,1)S(1)}, u32[]{:S(2)}, u32[]{:S(2)}) collective-permute-start(bf16[1,16,128,128]{3,2,1,0:T(8,128)(2,1)} %own_state.1), channel_id=1, source_target_pairs={{0,1},{1,2},{2,3},{3,4},{4,5},{5,6},{6,7},{7,8},{8,9},{9,10},{10,1... | collective-permute-start | bytes 1572872 | tf_op jit(solution)/shard_map/ppermute | solution.py:345
  9.0 1.3 collective-permute-start.1
  10.3 0.7 exponential_negate_fusion
  10.9 0.8 eq.15
  11.7 0.7 subtract_bitcast_fusion
  12.4 0.8 fusion.8
  13.2 0.1 copy.26.offset_ref
  13.3 0.1 copy.28
  13.4 0.0 collective-permute-done.2.low_conv
  13.4 0.0 collective-permute-done.3.high_conv
  13.4 0.0 collective-permute-done.low_state
  13.5 0.7 collective-permute-done.1.high_state
  14.2 0.0 copy-start.1
  14.2 1.0 copy-done.1
  15.2 0.0 copy-start.2
  15.2 1.0 copy-done.2
  16.2 0.0 copy-start.3
  16.2 0.9 copy-done.3
  17.2 0.0 copy-start.4
  17.2 0.8 copy-done.4
  18.0 0.0 copy-start.5
  18.0 0.8 copy-done.5
  18.8 0.0 copy-start.6
  18.8 0.7 copy-done.6
  19.4 5.6 %shard_map.181 = bf16[48,2048]{1,0:T(8,128)(2,1)S(1)} custom-call(s32[16,1]{1,0:T(8,128)S(1)} %copy.26.offset_ref, bf16[1,16,128,128]{3,2,1,0:T(8,128)(2,1)S(1)} %collective-permute-done.low_state, bf16[1,16,128,128]{3,2,1,0:T(8,128)(2,1)S(1)} %copy-done.1, bf16[1,16,128,128]{3,2,1,0:T(8,128)(2,1)S(1)} %collective-permute-done.1.high_state, ...), custom_call_target="tpu_custom_call" | custom-call | tf_op jit(solution)/shard_map/pallas_call | solution.py:351
  25.0 0.0 copy-start.7
  25.0 5.1 %multiply_reduce_fusion = (f32[48]{0:T(128)S(1)}, f32[48,2048]{1,0:T(8,128)S(1)}) fusion(bf16[48,2048]{1,0:T(8,128)(2,1)S(1)} %shard_map.181, bf16[2048,2048]{1,0:T(8,128)(2,1)} %param.31, bf16[48,2048]{1,0:T(8,128)(2,1)} %bitcast.25), kind=kOutput, calls=%fused_computation.9 | convolution fusion | flops 403046336 | bytes 9175232 | tf_op jit(solution)/shard_map/dot_general | solution.py:361
  30.1 0.0 copy-done.7
  30.1 0.1 multiply_convert_fusion
  30.3 0.0 copy-done
  30.3 0.3 fusion.9
  30.6 0.1 fusion.6
  30.7 0.8 concatenate.6
  31.5 123.2 %shard_map.182 = (f32[3,16,2048]{2,1,0:T(8,128)}, bf16[3,4,2,2,2,16,2176]{6,5,4,3,2,1,0:T(8,128)(2,1)}) custom-call(bf16[3,16,2176]{2,1,0:T(8,128)(2,1)} %bitcast.24, bf16[2048,256]{1,0:T(8,128)(2,1)} %bitcast.21, bf16[2048,256]{1,0:T(8,128)(2,1)} %bitcast.22, bf16[256,2048]{1,0:T(8,128)(2,1)} %bitcast.23), custom_call_target="tpu_custom_call" | custom-call | tf_op jit(solution)/shard_map/pallas_call | solution.py:307
  154.7 1.7 %fusion.4 = bf16[48,2048]{1,0:T(8,128)(2,1)} fusion(f32[48,2048]{1,0:T(8,128)S(1)} %get-tuple-element.10, f32[3,16,2048]{2,1,0:T(8,128)} %get-tuple-element.6), kind=kLoop, calls=%fused_computation.7 | loop fusion | flops 196608 | bytes 983040 | tf_op jit(solution)/shard_map/convert_element_type | solution.py:384
  (3 shorter events, 0.0 us)
Async XLA Ops:
  0.0 30.3 %copy-start = (bf16[2048,32]{0,1:T(8,128)(2,1)S(1)}, bf16[2048,32]{0,1:T(8,128)(2,1)}, u32[]{:S(2)}) copy-start(bf16[2048,32]{0,1:T(8,128)(2,1)} %param.33) | copy-start | bytes 393220
  0.0 13.4 %collective-permute-start.2 = (bf16[1,3,4096]{2,1,0:T(4,128)(2,1)}, bf16[1,3,4096]{2,1,0:T(4,128)(2,1)S(1)}, u32[]{:S(2)}, u32[]{:S(2)}) collective-permute-start(bf16[1,3,4096]{2,1,0:T(4,128)(2,1)} %own_conv.1), channel_id=1, source_target_pairs={{0,1},{1,2},{2,3},{3,4},{4,5},{5,6},{6,7},{7,8},{8,9},{9,10},{10,1... | collective-permute-start | bytes 73736 | tf_op jit(solution)/shard_map/ppermute | solution.py:343
  2.5 10.9 %collective-permute-start.3 = (bf16[1,3,4096]{2,1,0:T(4,128)(2,1)}, bf16[1,3,4096]{2,1,0:T(4,128)(2,1)S(1)}, u32[]{:S(2)}, u32[]{:S(2)}) collective-permute-start(bf16[1,3,4096]{2,1,0:T(4,128)(2,1)} %own_conv.1), channel_id=1, source_target_pairs={{1,0},{2,1},{3,2},{4,3},{5,4},{6,5},{7,6},{8,7},{9,8},{10,9},{11,1... | collective-permute-start | bytes 73736 | tf_op jit(solution)/shard_map/ppermute | solution.py:344
  3.8 9.7 %collective-permute-start = (bf16[1,16,128,128]{3,2,1,0:T(8,128)(2,1)}, bf16[1,16,128,128]{3,2,1,0:T(8,128)(2,1)S(1)}, u32[]{:S(2)}, u32[]{:S(2)}) collective-permute-start(bf16[1,16,128,128]{3,2,1,0:T(8,128)(2,1)} %own_state.1), channel_id=1, source_target_pairs={{0,1},{1,2},{2,3},{3,4},{4,5},{5,6},{6,7},{7,8},{8,9},{9,10},{10,1... | collective-permute-start | bytes 1572872 | tf_op jit(solution)/shard_map/ppermute | solution.py:345
  9.0 5.2 %collective-permute-start.1 = (bf16[1,16,128,128]{3,2,1,0:T(8,128)(2,1)}, bf16[1,16,128,128]{3,2,1,0:T(8,128)(2,1)S(1)}, u32[]{:S(2)}, u32[]{:S(2)}) collective-permute-start(bf16[1,16,128,128]{3,2,1,0:T(8,128)(2,1)} %own_state.1), channel_id=1, source_target_pairs={{1,0},{2,1},{3,2},{4,3},{5,4},{6,5},{7,6},{8,7},{9,8},{10,9},{11,1... | collective-permute-start | bytes 1572872 | tf_op jit(solution)/shard_map/ppermute | solution.py:346
  14.2 1.0 copy-start.1
  15.2 1.0 copy-start.2
  16.2 0.9 copy-start.3
  17.2 0.8 copy-start.4
  18.0 0.8 copy-start.5
  18.8 0.7 copy-start.6
  25.0 5.1 %copy-start.7 = (f32[2048]{0:T(1024)S(1)}, f32[2048]{0:T(1024)}, u32[]{:S(2)}) copy-start(f32[2048]{0:T(1024)} %param.32) | copy-start | bytes 24580

commit v4 on v3

--- a/solution.py
+++ b/solution.py
@@ -147,6 +147,44 @@
     )
 
 
+def neighbour_kernel(
+    count, state, conv, low_state, high_state, low_conv, high_conv, send_sem, recv_sem
+):
+    me = lax.axis_index("dev")
+    low, high = (me + count - 1) % count, (me + 1) % count
+    barrier = pltpu.get_barrier_semaphore()
+    for other in (low, high):
+        pl.semaphore_signal(
+            barrier, inc=1, device_id={"dev": other}, device_id_type=pl.DeviceIdType.MESH
+        )
+    pl.semaphore_wait(barrier, 2)
+    moves = (
+        (state, low_state, high), (state, high_state, low),
+        (conv, low_conv, high), (conv, high_conv, low),
+    )
+    copies = [
+        remote(source, target, send_sem.at[i], recv_sem.at[i], device)
+        for i, (source, target, device) in enumerate(moves)
+    ]
+    for copy in copies:
+        copy.start()
+    for copy in copies:
+        copy.wait()
+
+
+def neighbours(state, conv, count):
+    hbm = pl.BlockSpec(memory_space=pl.ANY)
+    kinds = [jax.ShapeDtypeStruct(a.shape, a.dtype) for a in (state, state, conv, conv)]
+    return pl.pallas_call(
+        functools.partial(neighbour_kernel, count),
+        out_shape=kinds,
+        in_specs=[hbm] * 2,
+        out_specs=[hbm] * 4,
+        scratch_shapes=[pltpu.SemaphoreType.DMA((4,)), pltpu.SemaphoreType.DMA((4,))],
+        compiler_params=pltpu.CompilerParams(collective_id=1, has_side_effects=True),
+    )(state, conv)
+
+
 def routed_kernel(
     count, in_ref, gate_ref, up_ref, down_ref, mixture_ref, out_ref, result, fetched, total,
     from_core, from_x, from_y, from_z, local_sem, send_sem, recv_sem, back_send, back_recv,
@@ -338,12 +376,9 @@
     count = lax.axis_size("dev")
     me = lax.axis_index("dev")
     rows = steps * slots
-    forward = [(i, i + 1) for i in range(count - 1)]
-    backward = [(i + 1, i) for i in range(count - 1)]
-    low_conv = lax.ppermute(conv_state, "dev", forward)
-    high_conv = lax.ppermute(conv_state, "dev", backward)
-    low_state = lax.ppermute(prompt_state, "dev", forward)
-    high_state = lax.ppermute(prompt_state, "dev", backward)
+    conv_lines = conv_state.reshape(-1, 128)
+    low_state, high_state, low_conv, high_conv = neighbours(prompt_state, conv_lines, count)
+    low_conv, high_conv = low_conv.reshape(conv_state.shape), high_conv.reshape(conv_state.shape)
     offset = (slot_prompt - (me - 1)).reshape(slots, 1)
     strength = jax.nn.sigmoid(beta_logit)
     retain = jnp.exp(-jnp.exp(decay_base) * jax.nn.softplus(decay_logit + decay_bias))

time: 157 us -> 157 us (level)
  the two profiles are of different devices: /device:TPU:0 before, /device:TPU:29 now
where the time goes in v4:
time: 157 us; the launch traced here: 156 us
  Pallas kernels  135 us (86%)
  local copies, waits for them, and re-layouts  12 us (8%)
  matrix products  5.38 us (3%)
  other arithmetic  4.11 us (3%)
    pallas_call x1, Pallas kernels, routed_sum(): pl.pallas_call(functools.partial(routed_kernel, count), out_shape=(jax.Sh...  114 us
    pallas_call x1, Pallas kernels, neighbours(): pl.pallas_call(functools.partial(neighbour_kernel, count), out_shape=kind...  15.4 us
    unnamed x20, local copies, waits for them, and re-layouts  7.3 us
    pallas_call x1, Pallas kernels, body(): pl.pallas_call(delta_kernel, out_shape=jax.ShapeDtypeStruct((rows, heads...  5.62 us
    dot_general x1, matrix products, body(): jnp.dot(gated, out_weight, preferred_element_type=jnp.float32)  5.07 us

profile of v4, /device:TPU:29, one launch (start us, length us, event | category | flops | bytes accessed | tf_op | source)
XLA Modules:
  0.0 156.3 jit_solution(2071450436240714372)
XLA Ops:
  0.0 0.0 copy-start
  0.0 0.7 subtract_bitcast_fusion
  0.7 0.7 exponential_negate_fusion
  1.4 0.1 copy.26.offset_ref
  1.4 0.8 eq.15
  2.3 0.1 copy.28
  2.4 1.4 reshape.42.conv
  3.8 0.8 fusion.8
  4.6 15.4 %shard_map.181 = (bf16[1,16,128,128]{3,2,1,0:T(8,128)(2,1)}, bf16[1,16,128,128]{3,2,1,0:T(8,128)(2,1)}, bf16[96,128]{1,0:T(8,128)(2,1)}, bf16[96,128]{1,0:T(8,128)(2,1)}) custom-call(bf16[1,16,128,128]{3,2,1,0:T(8,128)(2,1)} %own_state.1, bf16[96,128]{1,0:T(8,128)(2,1)} %reshape.42.conv), custom_call_target="tpu_custom_call" | custom-call | tf_op jit(solution)/shard_map/pallas_call | solution.py:178
  20.0 0.8 reshape.43.low_conv
  20.8 0.8 reshape.44.high_conv
  21.5 0.0 copy-start.1
  21.6 1.0 copy-done.1
  22.6 0.0 copy-start.2
  22.6 1.0 copy-done.2
  23.6 0.0 copy-start.3
  23.6 1.0 copy-done.3
  24.7 0.0 copy-start.4
  24.7 1.0 copy-done.4
  25.7 0.0 copy-start.5
  25.7 0.9 copy-done.5
  26.6 0.0 copy-start.6
  26.6 0.8 copy-done.6
  27.4 0.0 copy-start.7
  27.4 0.8 copy-done.7
  28.2 0.0 copy-start.8
  28.2 0.7 copy-done.8
  28.9 5.6 %shard_map.182 = bf16[48,2048]{1,0:T(8,128)(2,1)S(1)} custom-call(s32[16,1]{1,0:T(8,128)S(1)} %copy.26.offset_ref, bf16[1,16,128,128]{3,2,1,0:T(8,128)(2,1)S(1)} %copy-done.2, bf16[1,16,128,128]{3,2,1,0:T(8,128)(2,1)S(1)} %copy-done.1, bf16[1,16,128,128]{3,2,1,0:T(8,128)(2,1)S(1)} %copy-done.3, bf16[1,3,4096]{2,1,0:T(4,128)(2,1)S(1)} %reshape.43.low_conv, ...), custom_call_target="tpu_custom_call" | custom-call | tf_op jit(solution)/shard_map/pallas_call | solution.py:386
  34.5 0.0 copy-start.9
  34.5 5.1 %multiply_reduce_fusion = (f32[48]{0:T(128)S(1)}, f32[48,2048]{1,0:T(8,128)S(1)}) fusion(bf16[48,2048]{1,0:T(8,128)(2,1)S(1)} %shard_map.182, bf16[2048,2048]{1,0:T(8,128)(2,1)} %param.31, bf16[48,2048]{1,0:T(8,128)(2,1)} %bitcast.25), kind=kOutput, calls=%fused_computation.9 | convolution fusion | flops 403046336 | bytes 9175232 | tf_op jit(solution)/shard_map/dot_general | solution.py:396
  39.6 0.0 copy-done.9
  39.6 0.1 multiply_convert_fusion
  39.7 0.0 copy-done
  39.7 0.3 fusion.9
  40.0 0.1 fusion.6
  40.1 0.8 concatenate.6
  40.9 113.7 %shard_map.183 = (f32[3,16,2048]{2,1,0:T(8,128)}, bf16[3,4,2,2,2,16,2176]{6,5,4,3,2,1,0:T(8,128)(2,1)}) custom-call(bf16[3,16,2176]{2,1,0:T(8,128)(2,1)} %bitcast.24, bf16[2048,256]{1,0:T(8,128)(2,1)} %bitcast.21, bf16[2048,256]{1,0:T(8,128)(2,1)} %bitcast.22, bf16[256,2048]{1,0:T(8,128)(2,1)} %bitcast.23), custom_call_target="tpu_custom_call" | custom-call | tf_op jit(solution)/shard_map/pallas_call | solution.py:345
  154.6 1.7 %fusion.4 = bf16[48,2048]{1,0:T(8,128)(2,1)} fusion(f32[48,2048]{1,0:T(8,128)S(1)} %get-tuple-element.18, f32[3,16,2048]{2,1,0:T(8,128)} %get-tuple-element.14), kind=kLoop, calls=%fused_computation.7 | loop fusion | flops 196608 | bytes 983040 | tf_op jit(solution)/shard_map/convert_element_type | solution.py:419
  (3 shorter events, 0.0 us)
Async XLA Ops:
  0.0 39.7 %copy-start = (bf16[2048,32]{0,1:T(8,128)(2,1)S(1)}, bf16[2048,32]{0,1:T(8,128)(2,1)}, u32[]{:S(2)}) copy-start(bf16[2048,32]{0,1:T(8,128)(2,1)} %param.33) | copy-start | bytes 393220
  21.5 1.0 copy-start.1
  22.6 1.0 copy-start.2
  23.6 1.0 copy-start.3
  24.7 1.0 copy-start.4
  25.7 0.9 copy-start.5
  26.6 0.8 copy-start.6
  27.4 0.8 copy-start.7
  28.2 0.7 copy-start.8
  34.5 5.1 %copy-start.9 = (f32[2048]{0:T(1024)S(1)}, f32[2048]{0:T(1024)}, u32[]{:S(2)}) copy-start(f32[2048]{0:T(1024)} %param.32) | copy-start | bytes 24580
